TPU v7x, 256 devices: a whole 4x4x8 slice. The times are simulated.
256 devices in a mesh: blk: 32 (over z, x_hi, core), col: 8 (over x_lo, y).
Axes of the slice: x: 4 (x_hi: 2, x_lo: 2; x = x_hi * 2 + x_lo), y: 4, z: 8, core: 2. Of those that a mesh axis runs over, the one named last changes fastest.
Arguments:
- corner_blocks: bfloat16 [32, 65, 288, 288], P('blk'), may hold values from -0.046875 to 0.046875
- diag_shift: float32 [32, 2, 288], P('blk'), may hold values from 0.5 to 2
- sketch: bfloat16 [32, 2, 288, 1024], P('blk', None, None, 'col'), may hold values from -6 to 6
- panel_fold: int32 [32], replicated, may hold values from 0 to 31, each once
Outputs:
- first_image: float32 [32, 2, 288, 1024], P('blk', None, None, 'col')
- second_image: float32 [32, 2, 288, 1024], P('blk', None, None, 'col')
- gram: float32 [1024, 1024], P(None, 'col')
Inputs may be any that keep to these rules, and one draw needn't show every extreme that they name: panel_fold holds each of 0 to 31 once.
All inputs are finite; a program needn't handle non-finite values.
Results may differ from a plain program's by a relative error of at most 0.0034.
Values may be sent and summed in bfloat16 or wider, within the bound.
No kernel may reach another device: no remote copies, remote signals or barrier semaphores. Data moves between devices by JAX's collectives and lax.ppermute only.
A program may use at most 192 MiB of HBM per device.

v0:
```python
import jax
import jax.numpy as jnp
from jax import lax
from jax.sharding import PartitionSpec as P

ORDER = 18432


def local(corner_blocks, diag_shift, sketch, panel_fold):
    blk_count = lax.axis_size("blk")
    panels = 2 * blk_count
    anchor = panel_fold[lax.axis_index("blk")]
    blocks = corner_blocks[0]
    nblocks = blocks.shape[0]
    panel_width = blocks.shape[1]
    block_ids = jnp.arange(nblocks, dtype=jnp.int32)
    row_panel = jnp.where(block_ids <= anchor, anchor, panels - 1 - anchor)
    col_panel = jnp.where(block_ids <= anchor, block_ids, block_ids - anchor - 1)
    strict_mask = (jnp.arange(panel_width)[:, None] > jnp.arange(panel_width)[None, :]).astype(
        jnp.bfloat16
    )
    masked = blocks * jnp.where(
        (row_panel == col_panel)[:, None, None], strict_mask, jnp.ones_like(strict_mask)
    )
    slot_pairs = jnp.stack([panel_fold, panels - 1 - panel_fold], axis=1)
    slot_panels = slot_pairs.reshape(-1)
    slot_ids = jnp.arange(panels, dtype=jnp.int32)
    panel_ids = jnp.arange(panels, dtype=jnp.int32)
    owner_slot = jnp.sum(
        jnp.where(slot_panels[None, :] == panel_ids[:, None], slot_ids[None, :], 0), axis=1
    )
    col_slot = owner_slot[col_panel]
    lower_part = (block_ids <= anchor)[:, None, None]
    local_shift = diag_shift[0]

    def apply_corner(operand):
        gathered = lax.all_gather(operand[None], "blk", axis=0, tiled=True)
        columns = operand.shape[-1]
        flat_panels = gathered.reshape(panels, panel_width, columns)
        forward = jnp.einsum(
            "bij,bjk->bik", masked, flat_panels[col_slot], preferred_element_type=jnp.float32
        )
        upper_sum = jnp.sum(jnp.where(lower_part, forward, 0.0), axis=0)
        lower_sum = jnp.sum(jnp.where(lower_part, 0.0, forward), axis=0)
        local_part = jnp.stack([upper_sum, lower_sum])
        row_values = operand[jnp.where(block_ids <= anchor, 0, 1)]
        mirrored = jnp.einsum(
            "bij,bik->bjk", masked, row_values, preferred_element_type=jnp.float32
        )
        head_part = jnp.where(lower_part[:panels], mirrored[:panels], 0.0)
        padded = jnp.concatenate(
            [mirrored, jnp.zeros((panels - 1, panel_width, columns), jnp.float32)], axis=0
        )
        tail_part = lax.dynamic_slice_in_dim(padded, anchor + 1, panels, 0)
        natural = head_part + tail_part
        whole_term = natural[slot_panels].reshape(panels * panel_width, columns)
        returned = lax.psum_scatter(whole_term, "blk", scatter_dimension=0, tiled=True)
        returned = returned.reshape(2, panel_width, columns)
        return local_part + returned + local_shift[:, :, None] * operand.astype(jnp.float32)

    first_image = apply_corner(sketch[0])
    second_image = apply_corner(first_image.astype(jnp.bfloat16))
    second_rows = second_image.astype(jnp.bfloat16).reshape(2 * panel_width, second_image.shape[-1])
    full_second = lax.all_gather(second_rows, "col", axis=1, tiled=True)
    partial_gram = lax.dot_general(
        full_second, second_rows, (((0,), (0,)), ((), ())), preferred_element_type=jnp.float32
    )
    gram = lax.psum(partial_gram, "blk") / ORDER
    return (first_image[None], second_image[None], gram)


def solution(mesh):
    return jax.shard_map(
        local,
        mesh=mesh,
        in_specs=(
            P("blk", None, None, None),
            P("blk", None, None),
            P("blk", None, None, "col"),
            P(),
        ),
        out_specs=(P("blk", None, None, "col"), P("blk", None, None, "col"), P(None, "col")),
        check_vma=False,
    )
```

profile of v0, /device:TPU:1, one launch (start us, length us, event | category | flops | bytes accessed | tf_op | source)
XLA Modules:
  0.0 835.9 jit_solution(12097299064440545639)
XLA Ops:
  7.2 0.7 all-gather.4.cloned.1.call-update
  7.9 1.2 dynamic_slice.9
  11.1 0.7 subtract_bitcast_fusion
  11.8 0.7 pad_add_fusion
  12.7 0.7 fusion.9
  13.3 6.4 gather_fusion.2
  19.8 0.7 select_compare_fusion
  20.5 11.4 %fusion.15 = f32[65,288,128]{2,1,0:T(8,128)} fusion(bf16[65,288,128]{2,1,0:T(8,128)(2,1)} %gather_fusion.2, bf16[1,65,288,288]{3,2,1,0:T(8,128)(2,1)} %param.4, pred[65]{0:T(512)(128)(4,1)S(1)} %get-tuple-element.13, bf16[288,288]{1,0:T(8,128)(2,1)S(1)} %fusion.2), kind=kOutput, calls=%fused_computation.56 | convolution fusion | flops 1390970880 | bytes 25325632 | tf_op jit(solution)/shard_map/bij,bik->bjk/dot_general | solution.py:47
  31.8 12.0 %fusion = f32[64,288,128]{2,1,0:T(8,128)} fusion(s32[]{:T(128)S(6)} %select_n.119, f32[65,288,128]{2,1,0:T(8,128)} %fusion.15, pred[64]{0:T(512)(128)(4,1)S(1)} %bitcast.88), kind=kLoop, calls=%fused_computation.14 | loop fusion | flops 4718592 | bytes 28459076 | tf_op jit(solution)/shard_map/add | solution.py:55
  43.9 8.5 %gather_fusion.3 = f32[64,288,128]{2,1,0:T(8,128)} fusion(f32[64,288,128]{2,1,0:T(8,128)} %fusion, s32[1024]{0:T(1024)S(1)} %pad_clamp_fusion), kind=kCustom, calls=%fused_computation.3 | custom fusion | bytes 18874624 | tf_op jit(solution)/shard_map/gather | solution.py:56
  52.8 1.2 gather_fusion
  54.1 49.6 %all-gather.4.cloned.1.call-done = bf16[32,2,288,128]{3,2,1,0:T(8,128)(2,1)} async-done(((bf16[1,2,288,128]{3,2,1,0:T(8,128)(2,1)}), bf16[32,2,288,128]{3,2,1,0:T(8,128)(2,1)}) %all-gather.4.cloned.1.call-update) | async-done | bytes 4718608 | tf_op jit(solution)/shard_map/all_gather | solution.py:37
  103.7 8.2 gather_fusion.1
  111.9 10.2 %select_reduce_fusion.3 = (f32[288,128]{1,0:T(8,128)S(1)}, f32[288,128]{1,0:T(8,128)S(1)}) fusion(pred[65]{0:T(512)(128)(4,1)S(1)} %get-tuple-element.14, bf16[65,288,128]{2,1,0:T(8,128)(2,1)} %gather_fusion.1, bf16[1,65,288,288]{3,2,1,0:T(8,128)(2,1)} %param.4, pred[65]{0:T(512)(128)(4,1)S(1)} %get-tuple-element.13, bf16[288,288]{1,0:T(8,128)(2,1)S(1)} %fusion.2), kind=kOutput, calls=%fused_computation.13 | convolution fusion | flops 1400481792 | bytes 16035970 | tf_op jit(solution)/shard_map/bij,bjk->bik/dot_general | solution.py:40
  122.1 137.1 %reduce-scatter.3.cloned.1.call-done = f32[576,128]{1,0:T(8,128)} async-done(((f32[18432,128]{1,0:T(8,128)}), f32[576,128]{1,0:T(8,128)}) %reduce-scatter.3.cloned.1.call-update) | async-done | bytes 294928 | tf_op jit(solution)/shard_map/reduce_scatter | solution.py:57
  259.2 1.9 fusion.17
  261.3 1.1 pad_maximum_fusion
  262.5 5.5 gather_fusion.5
  268.0 11.3 %fusion.13 = f32[65,288,128]{2,1,0:T(8,128)} fusion(bf16[65,288,128]{2,1,0:T(8,128)(2,1)} %gather_fusion.5, bf16[1,65,288,288]{3,2,1,0:T(8,128)(2,1)} %param.4, pred[65]{0:T(512)(128)(4,1)S(1)} %get-tuple-element.13, bf16[288,288]{1,0:T(8,128)(2,1)S(1)} %fusion.2), kind=kOutput, calls=%fused_computation.54 | convolution fusion | flops 1390970880 | bytes 25325632 | tf_op jit(solution)/shard_map/bij,bik->bjk/dot_general | solution.py:47
  279.3 12.0 %fusion.1 = f32[64,288,128]{2,1,0:T(8,128)} fusion(s32[]{:T(128)S(6)} %select_n.119, f32[65,288,128]{2,1,0:T(8,128)} %fusion.13, pred[64]{0:T(512)(128)(4,1)S(1)} %bitcast.89), kind=kLoop, calls=%fused_computation.15 | loop fusion | flops 4718592 | bytes 28459076 | tf_op jit(solution)/shard_map/add | solution.py:55
  291.3 8.5 %gather_fusion.6 = f32[64,288,128]{2,1,0:T(8,128)} fusion(f32[64,288,128]{2,1,0:T(8,128)} %fusion.1, s32[1024]{0:T(1024)S(1)} %pad_clamp_fusion), kind=kCustom, calls=%fused_computation.6 | custom fusion | bytes 18874624 | tf_op jit(solution)/shard_map/gather | solution.py:56
  299.8 0.3 all-gather.8.cloned.1.call-start
  300.2 53.8 %all-gather.6.cloned.1.call-done = bf16[32,2,288,128]{3,2,1,0:T(8,128)(2,1)} async-done(((bf16[1,2,288,128]{3,2,1,0:T(8,128)(2,1)}), bf16[32,2,288,128]{3,2,1,0:T(8,128)(2,1)}) %all-gather.6.cloned.1.call-update) | async-done | bytes 4718608 | tf_op jit(solution)/shard_map/all_gather | solution.py:37
  354.0 8.2 gather_fusion.4
  362.2 10.1 %select_reduce_fusion.1 = (f32[288,128]{1,0:T(8,128)S(1)}, f32[288,128]{1,0:T(8,128)S(1)}) fusion(pred[65]{0:T(512)(128)(4,1)S(1)} %get-tuple-element.14, bf16[65,288,128]{2,1,0:T(8,128)(2,1)} %gather_fusion.4, bf16[1,65,288,288]{3,2,1,0:T(8,128)(2,1)} %param.4, pred[65]{0:T(512)(128)(4,1)S(1)} %get-tuple-element.13, bf16[288,288]{1,0:T(8,128)(2,1)S(1)} %fusion.2), kind=kOutput, calls=%fused_computation.11 | convolution fusion | flops 1400481792 | bytes 16035970 | tf_op jit(solution)/shard_map/bij,bjk->bik/dot_general | solution.py:40
  372.3 137.0 %reduce-scatter.5.cloned.1.call-done = f32[576,128]{1,0:T(8,128)} async-done(((f32[18432,128]{1,0:T(8,128)}), f32[576,128]{1,0:T(8,128)}) %reduce-scatter.5.cloned.1.call-update) | async-done | bytes 294928 | tf_op jit(solution)/shard_map/reduce_scatter | solution.py:57
  509.4 1.8 fusion.8
  511.2 39.3 %all-gather.8.cloned.1.call-done = bf16[576,1024]{1,0:T(8,128)(2,1)} async-done(((bf16[576,128]{1,0:T(8,128)(2,1)}), bf16[576,1024]{1,0:T(8,128)(2,1)}) %all-gather.8.cloned.1.call-update) | async-done | bytes 1179664 | tf_op jit(solution)/shard_map/all_gather | solution.py:64
  550.6 2.6 fusion.19
  553.2 1.8 fusion.4
  555.0 272.1 %all-reduce.4.cloned.1.call-done = f32[1024,128]{1,0:T(8,128)} async-done(((f32[1024,128]{1,0:T(8,128)}), f32[1024,128]{1,0:T(8,128)}) %all-reduce.4.cloned.1.call-update) | async-done | bytes 524304 | tf_op jit(solution)/shard_map/psum | solution.py:68
  827.1 1.9 broadcast_multiply_fusion
  (31 shorter events, 1.3 us)
Async XLA Ops:
  7.2 96.6 %all-gather.4.cloned.1.call-start = ((), (), s32[]{:S(2)}) async-start(), calls=%async_computation.2 | async-start | bytes 4866048 | tf_op jit(solution)/shard_map/all_gather | solution.py:37
  7.9 251.3 %reduce-scatter.3.cloned.1.call-start = ((), (), s32[]{:S(2)}) async-start(), calls=%async_computation.3 | async-start | bytes 9732096 | tf_op jit(solution)/shard_map/reduce_scatter | solution.py:57
  52.4 301.7 %all-gather.6.cloned.1.call-start = ((), (), s32[]{:S(2)}) async-start(), calls=%async_computation.4 | async-start | bytes 4866048 | tf_op jit(solution)/shard_map/all_gather | solution.py:37
  111.9 147.3 %copy-start = (bf16[1,2,288,128]{3,2,1,0:T(8,128)(2,1)S(1)}, bf16[1,2,288,128]{3,2,1,0:T(8,128)(2,1)}, u32[]{:S(2)}) copy-start(bf16[1,2,288,128]{3,2,1,0:T(8,128)(2,1)} %param.6) | copy-start | bytes 442372
  111.9 147.3 %copy-start.3 = (f32[1,2,288]{2,1,0:T(2,128)S(1)}, f32[1,2,288]{2,1,0:T(2,128)}, u32[]{:S(2)}) copy-start(f32[1,2,288]{2,1,0:T(2,128)} %param.5) | copy-start | bytes 6916
  261.1 248.3 %reduce-scatter.5.cloned.1.call-start = ((), (), s32[]{:S(2)}) async-start(), calls=%async_computation.5 | async-start | bytes 9732096 | tf_op jit(solution)/shard_map/reduce_scatter | solution.py:57
  299.8 250.7 %all-gather.8.cloned.1.call-start = ((), (), s32[]{:S(2)}) async-start(), calls=%async_computation.6 | async-start | bytes 1327104 | tf_op jit(solution)/shard_map/all_gather | solution.py:64
  362.2 147.2 %copy-start.1 = (f32[576,128]{1,0:T(8,128)S(1)}, f32[576,128]{1,0:T(8,128)}, u32[]{:S(2)}) copy-start(f32[576,128]{1,0:T(8,128)} %reduce-scatter.3.cloned.1.call-done) | copy-start | bytes 884740
  362.2 191.0 %copy-start.2 = (bf16[1,2,288,128]{3,2,1,0:T(8,128)(2,1)S(1)}, bf16[1,2,288,128]{3,2,1,0:T(8,128)(2,1)}, u32[]{:S(2)}) copy-start(bf16[1,2,288,128]{3,2,1,0:T(8,128)(2,1)} %get-tuple-element.7) | copy-start | bytes 442372
  511.2 316.0 %all-reduce.4.cloned.1.call-start = ((), (), s32[]{:S(2)}) async-start(), calls=%async_computation.7 | async-start | bytes 1048576 | tf_op jit(solution)/shard_map/psum | solution.py:68
Sparse Core Ops, SparseCore 0:
  10.8 92.9 all-gather.3
  108.2 150.9 reduce-scatter.2
  262.9 91.0 all-gather.5
  359.0 150.3 reduce-scatter.4
  511.3 39.2 all-gather.7
  553.6 273.5 all-reduce.3
where the time goes:
time: 836 us
  waiting for transfers between devices  690 us (83%)
  local copies, waits for them, and re-layouts  48.1 us (6%)
  matrix products  45.6 us (5%)
  other arithmetic  35.3 us (4%)
  between operations  16.2 us (2%)
    reduce_scatter x2, waiting for transfers between devices, apply_corner(): lax.psum_scatter(whole_term, 'blk', scatter_dimension=0, tiled=True)  274 us
    psum x1, waiting for transfers between devices, local(): gram = lax.psum(partial_gram, 'blk') / ORDER  272 us
    all_gather x2, waiting for transfers between devices, apply_corner(): gathered = lax.all_gather(operand[None], 'blk', axis=0, tiled=True)  103 us
    all_gather x1, waiting for transfers between devices, local(): full_second = lax.all_gather(second_rows, 'col', axis=1, tiled=True)  39.3 us
    add x2, other arithmetic, apply_corner(): natural = head_part + tail_part  24 us
    dot_general x2, matrix products, apply_corner(): jnp.einsum('bij,bik->bjk', masked, row_values, preferred_element_type=jnp...  22.7 us
    dot_general x2, matrix products, apply_corner(): jnp.einsum('bij,bjk->bik', masked, flat_panels[col_slot], preferred_eleme...  20.3 us
    gather x2, local copies, waits for them, and re-layouts, apply_corner(): whole_term = natural[slot_panels].reshape(panels * panel_width, columns)  17 us
  transfers between devices with their start and end apart: 6, of which 6 were waited for; matrix products, arithmetic and copies ran while one was open for 14% of the time, Pallas kernels for 0%

commit v1 on v0

v1 whole, which is shorter than its diff:
```python
import functools

import jax
import jax.numpy as jnp
import numpy as np
from jax import lax
from jax.experimental import pallas as pl
from jax.experimental.pallas import tpu as pltpu
from jax.sharding import Mesh, PartitionSpec as P

ORDER = 18432
PANELS = 64
PANEL = 288
NZ = 8
ALL = ("z", "xh", "core", "xl", "y")
BLK = ("z", "xh", "core")
COL = ("xl", "y")
FLIP = [(0, 1), (1, 0)]
WINDOW = 40
SHARE = 72


def hop(x, k):
    return lax.ppermute(x, "z", [(i, (i + k) % NZ) for i in range(NZ)])


def ring_gather(x):
    half = x.shape[0] // 2 + 4
    up, down = [x], [x]
    for _ in range(3):
        up.append(hop(up[-1], 1))
        down.append(hop(down[-1], -1))
    far = jnp.concatenate([hop(up[-1][:half], 1), hop(down[-1][half:], -1)])
    return up + [far] + down[:0:-1]


def shares():
    out = []
    for c in range(NZ):
        base, odd = SHARE * (c >> 1), c % 2
        out.append((base + 40 * odd, 40 - 8 * odd, base + 32 * odd, 32 + 8 * odd))
    return out


def row_order():
    order = []
    for s0, n0, s1, n1 in shares():
        order += list(range(s0 // 8, (s0 + n0) // 8))
        order += list(range((PANEL + s1) // 8, (PANEL + s1 + n1) // 8))
    return np.array(order)


def split_rows(x):
    x = x.reshape((SHARE, 8) + x.shape[1:])
    x = jnp.take(x, row_order(), axis=0)
    return x.reshape((NZ, SHARE) + x.shape[2:])


def merge_rows(x):
    x = x.reshape((SHARE, 8) + x.shape[2:])
    x = jnp.take(x, np.argsort(row_order()), axis=0)
    return x.reshape((2 * PANEL,) + x.shape[2:])


def window_kernel(fold, place, blocks, out, held, sems):
    anchor = fold[place[2]]

    def copies(n):
        rows = pl.ds(pl.multiple_of(place[0], 16), WINDOW + 8)
        return [
            pltpu.make_async_copy(blocks.at[index, rows, :], held.at[n, k], sems.at[k])
            for k, index in enumerate(block_pair(anchor, fold[n]))
        ]

    def start(n, carry):
        for copy in copies(n):
            copy.start()
        return carry

    def wait(n, carry):
        for copy in copies(n):
            copy.wait()
        return carry

    def pack(m, carry):
        for k in range(4):
            n = 4 * m + k
            rows = jnp.concatenate([held[n, k].astype(jnp.float32) for k in range(2)], axis=1)
            out[n] = jnp.where(place[1] == 1, rows[8:], rows[:WINDOW]).astype(out.dtype)
        return carry

    lax.fori_loop(0, 32, start, 0)
    lax.fori_loop(0, 32, wait, 0)
    lax.fori_loop(0, 8, pack, 0)


def block_windows(blocks, fold, start, pair):
    place = jnp.stack([start & -16, (start >> 3) & 1, pair])
    return pl.pallas_call(
        window_kernel,
        in_specs=[pl.BlockSpec(memory_space=pltpu.SMEM)] * 2 + [pl.BlockSpec(memory_space=pl.ANY)],
        out_specs=pl.BlockSpec(memory_space=pltpu.VMEM),
        out_shape=jax.ShapeDtypeStruct((32, WINDOW, 2 * PANEL), blocks.dtype),
        scratch_shapes=[
            pltpu.VMEM((32, 2, WINDOW + 8, PANEL), blocks.dtype),
            pltpu.SemaphoreType.DMA((2,)),
        ],
        compiler_params=pltpu.CompilerParams(vmem_limit_bytes=56 * 2**20),
        cost_estimate=pl.CostEstimate(flops=0, bytes_accessed=6 * 2**20, transcendentals=0),
    )(fold, place, blocks)


def block_pair(anchor, partner):
    return partner + anchor + 1, jnp.where(anchor < partner, PANELS - partner + anchor, partner)


def product_kernel(by_rows, places, weights, *refs):
    pieces, out = refs[:32], refs[-1]
    x = jnp.concatenate([piece[...] for piece in pieces], axis=0)
    y = lax.dot_general(
        weights[...], x, (((0,), (0,)), ((), ())), preferred_element_type=jnp.float32
    )
    if by_rows:
        for c, (s0, n0, s1, n1) in enumerate(shares()):
            share = jnp.concatenate([y[s0 : s0 + n0], y[PANEL + s1 : PANEL + s1 + n1]])
            out[c] = share.astype(out.dtype)
    else:
        extra = jnp.concatenate([piece[...] for piece in refs[32:-1]], axis=0)
        for c in range(out.shape[0]):
            columns = slice(128 * c, 128 * c + 128)
            out[c, : 2 * PANEL] = y[:, columns].astype(out.dtype)
            out[c, 2 * PANEL :] = extra[:, columns]


def product(weights, places, pieces, extra=(), width=256):
    depth, rows = weights.shape
    by_rows = not extra
    if by_rows:
        shape, block, place = (NZ, SHARE, 1024), (NZ, SHARE, width), lambda i, at: (0, 0, i)
    else:
        height = rows + SHARE * len(extra)
        shape, block = (NZ, height, 128), (width // 128, height, 128)
        place = lambda i, at: (i, 0, 0)

    def slab(entry):
        if entry is None:
            return pl.BlockSpec((SHARE, width), lambda i, at: (0, i))
        return pl.BlockSpec((None, SHARE, width), lambda i, at: (at[entry], 0, i))

    operands = list(pieces) + [(x, None) for x in extra]
    return pl.pallas_call(
        functools.partial(product_kernel, by_rows),
        grid_spec=pltpu.PrefetchScalarGridSpec(
            num_scalar_prefetch=1,
            grid=(1024 // width,),
            in_specs=[pl.BlockSpec((depth, rows), lambda i, at: (0, 0))]
            + [slab(entry) for _, entry in operands],
            out_specs=pl.BlockSpec(block, place),
        ),
        out_shape=jax.ShapeDtypeStruct(shape, jnp.bfloat16),
        compiler_params=pltpu.CompilerParams(vmem_limit_bytes=60 * 2**20),
        cost_estimate=pl.CostEstimate(
            flops=2 * depth * rows * 1024, bytes_accessed=9 * 2**20, transcendentals=0
        ),
    )(places, weights, *[x for x, _ in operands])


def align(odd, k0, k1):
    even = jnp.concatenate([k0, k1[:32]], axis=0)
    late = jnp.concatenate([k0[8:], k1], axis=0)
    return jnp.where(odd == 1, late, even)


def own_kernel(below, odd, first, second, diagonal, out):
    def place(n):
        t1 = first[n].astype(jnp.float32)
        t2 = second[n].astype(jnp.float32)
        under = below[n] == 1
        zero = jnp.zeros_like(t2)
        k00 = jnp.where(n == 0, diagonal[0], jnp.where(under, zero, t2))
        k11 = jnp.where(n == 0, diagonal[1], jnp.where(under, t2, zero))
        k0 = jnp.concatenate([k00, t1], axis=1)
        k1 = jnp.concatenate([zero, k11], axis=1)
        out[n] = align(odd[0], k0, k1).astype(out.dtype)

    def step(m, carry):
        for k in range(4):
            place(4 * m + k)
        return carry

    lax.fori_loop(0, 8, step, 0)


def merge_kernel(order, below, odd, taken, own, out):
    left = lax.broadcasted_iota(jnp.int32, (WINDOW, 2 * PANEL), 1) < PANEL

    def place(n):
        r = taken[order[n]].astype(jnp.float32)
        turned = jnp.concatenate([r[:, PANEL:], r[:, :PANEL]], axis=1)
        under = below[n] == 1
        k0 = jnp.where(left, jnp.where(under, turned, 0.0), 0.0)
        k1 = jnp.where(left, r, jnp.where(under | (n == 0), 0.0, r))
        out[n] = own[n] + align(odd[0], k0, k1).astype(out.dtype)

    def step(m, carry):
        for k in range(8):
            place(8 * m + k)
        return carry

    lax.fori_loop(0, 4, step, 0)


def on_device(kernel, scalars, arrays):
    return pl.pallas_call(
        kernel,
        in_specs=[pl.BlockSpec(memory_space=pltpu.SMEM)] * len(scalars)
        + [pl.BlockSpec(memory_space=pltpu.VMEM)] * len(arrays),
        out_specs=pl.BlockSpec(memory_space=pltpu.VMEM),
        out_shape=jax.ShapeDtypeStruct((32, SHARE, 2 * PANEL), jnp.bfloat16),
        compiler_params=pltpu.CompilerParams(vmem_limit_bytes=56 * 2**20),
        cost_estimate=pl.CostEstimate(flops=0, bytes_accessed=6 * 2**20, transcendentals=0),
    )(*scalars, *arrays)


def local(corner_blocks, diag_shift, sketch, panel_fold):
    z = lax.axis_index("z")
    core = lax.axis_index("core")
    xh = lax.axis_index("xh")
    e = xh * 2 + core
    c = lax.axis_index("xl") * 4 + lax.axis_index("y")
    odd = c & 1
    anchor = panel_fold[z * 4 + e]
    blocks = corner_blocks[0]
    start = SHARE * (c >> 1) + 32 * odd

    def to_shares(x):
        x = split_rows(x)
        x = lax.all_to_all(jnp.concatenate([x, x]), ("xh",) + COL, 0, 0, tiled=True)
        x = jnp.swapaxes(x.reshape(2, NZ, SHARE, 128), 1, 2)
        return x.reshape(2, SHARE, NZ * 128)

    def gather_operand(x):
        far = lax.ppermute(x, "xh", FLIP)
        near, far = ring_gather(x), ring_gather(far)
        out = []
        for pair in zip(near, far):
            for p in pair:
                out += [p, lax.ppermute(p, "core", FLIP)]
        return [(p, None) for p in out]

    pair = to_shares(sketch[0].reshape(2 * PANEL, 128))
    share = lax.dynamic_index_in_dim(pair, xh, 0, keepdims=False)
    sent = block_windows(blocks, panel_fold, start, z * 4 + e)
    gathered = lax.all_gather(pair, "z", axis=0, tiled=True)
    taken = lax.all_to_all(sent, BLK, 0, 0, tiled=True)

    blocks, pair = lax.optimization_barrier((blocks, pair))
    down = lax.dynamic_slice(blocks, (0, 0, start), (PANELS + 1, PANEL, WINDOW))
    down = jnp.swapaxes(down, 1, 2)

    hops, turn = jnp.arange(NZ)[:, None], jnp.arange(4)[None, :]
    places = ((z - hops) % NZ * 2 + (xh ^ jnp.arange(2)[None, :])).reshape(-1)
    order = (((z - hops) % NZ) * 4 + (e ^ turn)).reshape(-1)
    partner = panel_fold[order]
    below = (anchor < partner).astype(jnp.int32)

    row = start + lax.broadcasted_iota(jnp.int32, (WINDOW, PANEL), 0)
    column = lax.broadcasted_iota(jnp.int32, (WINDOW, PANEL), 1)

    def diagonal(index):
        low = lax.dynamic_slice(blocks, (index, start, 0), (1, WINDOW, PANEL))[0]
        high = lax.dynamic_index_in_dim(down, index, 0, keepdims=False)
        zero = jnp.zeros_like(low)
        return jnp.where(row > column, low, jnp.where(row < column, high, zero))

    diagonals = jnp.stack([diagonal(anchor), diagonal(PANELS)]).astype(jnp.float32)
    own = [jnp.take(down, index, axis=0) for index in block_pair(anchor, partner)]
    odd = odd.reshape(1)
    own = on_device(own_kernel, (below, odd), (*own, diagonals))
    gathered, own, order, places = lax.optimization_barrier((gathered, own, order, places))
    swapped = lax.ppermute(gathered, "core", FLIP)
    pieces = [
        (x, 2 * t + part) for t in range(NZ) for part in range(2) for x in (gathered, swapped)
    ]
    weights = on_device(merge_kernel, (order, below, odd), (taken, own))
    weights = weights.reshape(32 * SHARE, 2 * PANEL)

    shift_rows = diag_shift[0].reshape(2 * PANEL, 1)
    shift_share = lax.dynamic_index_in_dim(split_rows(shift_rows), c, 0, keepdims=False)

    parts = lax.all_to_all(product(weights, places, pieces), COL, 0, 0, tiled=True)
    share = jnp.sum(parts.astype(jnp.float32), axis=0) + shift_share * share.astype(jnp.float32)
    rounded = lax.reduce_precision(share, 8, 7)
    high, low = rounded.astype(jnp.bfloat16), (share - rounded).astype(jnp.bfloat16)
    pieces = gather_operand(high)
    parts = lax.all_to_all(product(weights, places, pieces, (high, low)), COL, 0, 0, tiled=True)
    x = merge_rows(parts[:, 2 * PANEL : 2 * PANEL + SHARE]).astype(jnp.float32)
    first = x + merge_rows(parts[:, 2 * PANEL + SHARE :]).astype(jnp.float32)
    second = jnp.sum(parts[:, : 2 * PANEL].astype(jnp.float32), axis=0) + shift_rows * x
    x = second.astype(jnp.bfloat16)

    rows = lax.all_to_all(jnp.broadcast_to(x, (NZ,) + x.shape), COL, 0, 0, tiled=True)
    rows, first, second = lax.optimization_barrier((rows, first, second))
    part = lax.dot_general(rows, x, (((1,), (0,)), ((), ())), preferred_element_type=jnp.float32)
    part = part.reshape(2, 512, 128)
    mine = lax.dynamic_index_in_dim(part, core, 0, keepdims=False)
    theirs = lax.dynamic_index_in_dim(part, 1 - core, 0, keepdims=False)
    mine = mine + lax.ppermute(theirs, "core", FLIP)
    mine = jnp.sum(lax.all_to_all(mine.reshape(NZ, 64, 128), "z", 0, 0, tiled=True), axis=0)
    mine = (mine + lax.ppermute(mine, "xh", FLIP)) / ORDER
    mine = lax.all_to_all(jnp.broadcast_to(mine, (NZ,) + mine.shape), "z", 0, 0, tiled=True)
    mine = mine.reshape(512, 128)
    other = lax.ppermute(mine, "core", FLIP)
    gram = jnp.where(core == 0, jnp.concatenate([mine, other]), jnp.concatenate([other, mine]))
    return first.reshape(1, 2, PANEL, 128), second.reshape(1, 2, PANEL, 128), gram


def solution(mesh):
    fine = Mesh(mesh.devices.reshape(NZ, 2, 2, 2, 4), ALL)
    return jax.shard_map(
        local,
        mesh=fine,
        in_specs=(P(BLK, None, None, None), P(BLK, None, None), P(BLK, None, None, COL), P()),
        out_specs=(P(BLK, None, None, COL), P(BLK, None, None, COL), P(None, COL)),
        check_vma=False,
    )
```

time: 836 us -> 288 us (0.34)
  waiting for transfers between devices: 690 us -> 83.5 us
  starting transfers between devices: 0.9 us -> 66.8 us
  matrix products: 45.6 us -> 0.67 us
  blocking collectives: 0 us -> 42.5 us
  Pallas kernels: 0 us -> 31.6 us
  other arithmetic: 35.3 us -> 9.53 us
  local copies, waits for them, and re-layouts: 48.1 us -> 35.3 us
    reduce_scatter x2 -> x0, waiting for transfers between devices: 274 us -> none  [apply_corner(): lax.psum_scatter(whole_term, 'blk', scatter_dimension=0, tiled=True)]
    psum x1 -> x0, waiting for transfers between devices: 272 us -> none  [local(): gram = lax.psum(partial_gram, 'blk') / ORDER]
    all_gather x3 -> x1, waiting for transfers between devices: 143 us -> 18.4 us  [local(): gathered = lax.all_gather(pair, 'z', axis=0, tiled=True)]
    all_to_all x0 -> x4, waiting for transfers between devices: none -> 52.6 us  [the longest x1 19.5 us: local(): lax.all_to_all(product(weights, places, pieces, (high, low)), COL, 0, 0,...]
    dot_general x5 -> x1, matrix products: 45.6 us -> 0.67 us  [local(): lax.dot_general(rows, x, (((1,), (0,)), ((), ())), preferred_element_type...]
    ppermute x0 -> x37, starting transfers between devices: none -> 43.9 us  [the longest x16 19.1 us: hop(): return lax.ppermute(x, 'z', [(i, (i + k) % NZ) for i in range(NZ)])]
    all_to_all x0 -> x3, blocking collectives: none -> 42.5 us  [the longest x1 15.8 us: local(): lax.all_to_all(mine.reshape(NZ, 64, 128), 'z', 0, 0, tiled=True)]
    gather x7 -> x8, local copies, waits for them, and re-layouts: 46.4 us -> 5.73 us  [the longest x2 2.43 us: local(): jnp.take(down, index, axis=0)]
  transfers between devices with their start and end apart: 6 -> 42, of which waited for: 6 -> 16; matrix products, arithmetic and copies ran while one was open for 14% -> 12% of each run, Pallas kernels for 0% -> 5%
where the time goes in v1:
time: 288 us; the launch traced here: 287 us
  waiting for transfers between devices  83.5 us (29%)
  starting transfers between devices  66.8 us (23%)
  blocking collectives  42.5 us (15%)
  local copies, waits for them, and re-layouts  35.3 us (12%)
  Pallas kernels  31.6 us (11%)
  between operations  16.7 us (6%)
  other arithmetic  9.53 us (3%)
    optimization_barrier x1, local copies, waits for them, and re-layouts, local(): blocks, pair = lax.optimization_barrier((blocks, pair))  19.6 us
    all_to_all x1, waiting for transfers between devices, local(): lax.all_to_all(product(weights, places, pieces, (high, low)), COL, 0, 0,...  19.5 us
    ppermute x16, starting transfers between devices, hop(): return lax.ppermute(x, 'z', [(i, (i + k) % NZ) for i in range(NZ)])  19.1 us
    all_gather x1, waiting for transfers between devices, local(): gathered = lax.all_gather(pair, 'z', axis=0, tiled=True)  18.4 us
    pallas_call x2, Pallas kernels, product(): pl.pallas_call(functools.partial(product_kernel, by_rows), grid_spec=pltp...  18.1 us
    all_to_all x1, waiting for transfers between devices, local(): lax.all_to_all(jnp.broadcast_to(x, (NZ,) + x.shape), COL, 0, 0, tiled=True)  16.3 us
    all_to_all x1, blocking collectives, local(): lax.all_to_all(mine.reshape(NZ, 64, 128), 'z', 0, 0, tiled=True)  15.8 us
    all_to_all x1, waiting for transfers between devices, local(): lax.all_to_all(product(weights, places, pieces), COL, 0, 0, tiled=True)  15.6 us
  transfers between devices with their start and end apart: 42, of which 16 were waited for; matrix products, arithmetic and copies ran while one was open for 12% of the time, Pallas kernels for 5%

profile of v1, /device:TPU:1, one launch (start us, length us, event | category | flops | bytes accessed | tf_op | source)
XLA Modules:
  0.0 286.7 jit_solution(11572709799438058971)
XLA Ops:
  8.8 14.9 %all_to_all.35 = bf16[16,72,128]{2,1,0:T(8,128)(2,1)S(1)} all-to-all(bf16[16,72,128]{2,1,0:T(8,128)(2,1)S(1)} %pad_maximum_fusion), channel_id=1, replica_groups=mesh['z'=8,'xh'=2,'core'=2,'xl'=2,'y'=4] {'xh','xl','y'}, dimensions={0} | all-to-all | bytes 589824 | tf_op jit(solution)/shard_map/all_to_all | solution.py:238
  25.2 4.4 %shard_map.104 = bf16[32,40,576]{2,1,0:T(8,128)(2,1)} custom-call(s32[32]{0:T(128)} %fold.1, s32[3]{0:T(128)} %pad_add_fusion.place, bf16[65,288,288]{2,1,0:T(8,128)(2,1)} %bitcast.68), custom_call_target="tpu_custom_call" | custom-call | bytes 6291456 | tf_op jit(solution)/shard_map/pallas_call | solution.py:99
  29.6 11.6 %all-to-all-start.1 = ((bf16[32,40,576]{2,1,0:T(8,128)(2,1)}), bf16[32,40,576]{2,1,0:T(8,128)(2,1)}, u32[]{:S(2)}, u32[]{:S(2)}) async-start(bf16[32,40,576]{2,1,0:T(8,128)(2,1)} %shard_map.104), calls=%async_computation.1 | async-start | bytes 3276800 | tf_op jit(solution)/shard_map/all_to_all | solution.py:255
  47.1 19.6 %copy.19 = bf16[65,288,288]{1,2,0:T(8,128)(2,1)} copy(bf16[65,288,288]{2,1,0:T(8,128)(2,1)} %bitcast.69) | data formatting | bytes 21565440 | tf_op jit(solution)/shard_map/optimization_barrier | solution.py:257
  66.7 1.8 dynamic-slice_bitcast_fusion
  74.8 4.2 %shard_map.103.own = bf16[32,72,576]{2,1,0:T(8,128)(2,1)} custom-call(s32[32]{0:T(128)} %get-tuple-element.36.below, s32[1]{0:T(128)} %bitcast.6.odd, bf16[32,40,288]{2,1,0:T(8,128)(2,1)} %broadcast_select_fusion.1.first, bf16[32,40,288]{2,1,0:T(8,128)(2,1)} %broadcast_select_fusion.second, f32[2,40,288]{2,1,0:T(8,128)} %maximum_convert_fusion.diagonal), custom_call_target="tpu_custom_call" | custom-call | bytes 6291456 | tf_op jit(solution)/shard_map/pallas_call | solution.py:214
  79.1 18.4 %all-gather.2.cloned.1.call-done.refs_0_.refs_2_.refs_4_.refs_6_.refs_8_.refs_10_.refs_12_.refs_14_.refs_16_.refs_18_.refs_20_.refs_22_.refs_24_.refs_26_.refs_28_.refs_30_ = bf16[16,72,1024]{2,1,0:T(8,128)(2,1)} async-done(((bf16[2,72,1024]{2,1,0:T(8,128)(2,1)}), bf16[16,72,1024]{2,1,0:T(8,128)(2,1)}) %all-gather.2.cloned.1.call-update) | async-done | bytes 2359312 | tf_op jit(solution)/shard_map/all_gather | solution.py:254
  100.3 4.9 %shard_map.105 = bf16[32,72,576]{2,1,0:T(8,128)(2,1)} custom-call(s32[32]{0:T(128)} %add.199.order, s32[32]{0:T(128)} %get-tuple-element.36.below, s32[1]{0:T(128)} %bitcast.6.odd, bf16[32,40,576]{2,1,0:T(8,128)(2,1)} %all-to-all-done.1.taken, bf16[32,72,576]{2,1,0:T(8,128)(2,1)} %shard_map.103.own), custom_call_target="tpu_custom_call" | custom-call | bytes 6291456 | tf_op jit(solution)/shard_map/pallas_call | solution.py:214
  106.6 9.8 %shard_map.106 = bf16[8,72,1024]{2,1,0:T(8,128)(2,1)} custom-call(s32[16]{0:T(128)} %add.203.places, bf16[2304,576]{1,0:T(8,128)(2,1)} %bitcast.71, bf16[16,72,1024]{2,1,0:T(8,128)(2,1)} %all-gather.2.cloned.1.call-done.refs_0_.refs_2_.refs_4_.refs_6_.refs_8_.refs_10_.refs_12_.refs_14_.refs_16_.refs_18_.refs_20_.refs_22_.refs_24_.refs_26_.refs_28_.refs_30_, ...), custom_call_target="tpu_custom_call" | custom-call | flops 2717908992 | bytes 9437184 | tf_op jit(solution)/shard_map/pallas_call | solution.py:151
  116.4 4.0 %all-to-all-start.2 = ((bf16[8,72,1024]{2,1,0:T(8,128)(2,1)}), bf16[8,72,1024]{2,1,0:T(8,128)(2,1)S(1)}, u32[]{:S(2)}, u32[]{:S(2)}) async-start(bf16[8,72,1024]{2,1,0:T(8,128)(2,1)} %shard_map.106), calls=%async_computation.2 | async-start | bytes 2359296 | tf_op jit(solution)/shard_map/all_to_all | solution.py:291
  121.1 15.6 %all-to-all-done.2 = bf16[8,72,1024]{2,1,0:T(8,128)(2,1)S(1)} async-done(((bf16[8,72,1024]{2,1,0:T(8,128)(2,1)}), bf16[8,72,1024]{2,1,0:T(8,128)(2,1)S(1)}, u32[]{:S(2)}, u32[]{:S(2)}) %all-to-all-start.2) | async-done | bytes 1179680 | tf_op jit(solution)/shard_map/all_to_all | solution.py:291
  137.8 2.1 collective-permute-start.2
  140.3 2.2 collective-permute-start.17
  143.9 2.7 collective-permute-start.23
  146.6 2.7 collective-permute-start.18
  149.3 2.7 collective-permute-start.24
  152.8 3.9 %collective-permute-start.1 = (bf16[72,1024]{1,0:T(8,128)(2,1)S(1)}, bf16[72,1024]{1,0:T(8,128)(2,1)S(1)}, u32[]{:S(2)}, u32[]{:S(2)}) collective-permute-start(bf16[72,1024]{1,0:T(8,128)(2,1)S(1)} %get-tuple-element.32.refs_0_.refs_32_), channel_id=1, source_target_pairs={{0,8},{8,0},{1,9},{9,1},{2,10},{10,2},{3,11},{11,3},{4,12},{12,4},... | collective-permute-start | bytes 442376 | tf_op jit(solution)/shard_map/ppermute | solution.py:248
  156.7 3.0 %collective-permute-start.19 = (bf16[72,1024]{1,0:T(8,128)(2,1)S(1)}, bf16[72,1024]{1,0:T(8,128)(2,1)S(1)}, u32[]{:S(2)}, u32[]{:S(2)}) collective-permute-start(bf16[72,1024]{1,0:T(8,128)(2,1)S(1)} %collective-permute-done.18.refs_24_), channel_id=1, source_target_pairs={{0,224},{32,0},{64,32},{96,64},{128,96},{160,128},{192,160},{224,1... | collective-permute-start | bytes 442376 | tf_op jit(solution)/shard_map/ppermute | solution.py:24
  160.3 2.7 collective-permute-start.25
  163.1 2.1 collective-permute-start.32
  165.3 3.1 %collective-permute-done.16 = bf16[40,1024]{1,0:T(8,128)(2,1)S(1)} collective-permute-done((bf16[40,1024]{1,0:T(8,128)(2,1)S(1)}, bf16[40,1024]{1,0:T(8,128)(2,1)S(1)}, u32[]{:S(2)}, u32[]{:S(2)}) %collective-permute-start.16) | collective-permute-done | bytes 81952 | tf_op jit(solution)/shard_map/ppermute | solution.py:24
  174.0 2.3 collective-permute-start.7
  182.7 8.4 %shard_map.107 = bf16[8,720,128]{2,1,0:T(8,128)(2,1)} custom-call(s32[16]{0:T(128)} %add.203.places, bf16[2304,576]{1,0:T(8,128)(2,1)} %bitcast.72, bf16[72,1024]{1,0:T(8,128)(2,1)} %copy-done.6, bf16[72,1024]{1,0:T(8,128)(2,1)} %copy-done.24, bf16[72,1024]{1,0:T(8,128)(2,1)} %copy-done.15, bf16[72,1024]{1,0:T(8,128)(2,1)} %copy-done.25, ...), custom_call_target="tpu_custom_call" | custom-call | flops 2717908992 | bytes 9437184 | tf_op jit(solution)/shard_map/pallas_call | solution.py:151
  191.1 3.7 %all-to-all-start.3 = ((bf16[8,720,128]{2,1,0:T(8,128)(2,1)}), bf16[8,720,128]{2,1,0:T(8,128)(2,1)S(1)}, u32[]{:S(2)}, u32[]{:S(2)}) async-start(bf16[8,720,128]{2,1,0:T(8,128)(2,1)} %shard_map.107), calls=%async_computation.3 | async-start | bytes 2949120 | tf_op jit(solution)/shard_map/all_to_all | solution.py:296
  194.8 19.5 %all-to-all-done.3 = bf16[8,720,128]{2,1,0:T(8,128)(2,1)S(1)} async-done(((bf16[8,720,128]{2,1,0:T(8,128)(2,1)}), bf16[8,720,128]{2,1,0:T(8,128)(2,1)S(1)}, u32[]{:S(2)}, u32[]{:S(2)}) %all-to-all-start.3) | async-done | bytes 1474592 | tf_op jit(solution)/shard_map/all_to_all | solution.py:296
  217.8 3.6 %all-to-all-start.4 = ((bf16[8,576,128]{2,1,0:T(8,128)(2,1)}), bf16[8,576,128]{2,1,0:T(8,128)(2,1)S(1)}, u32[]{:S(2)}, u32[]{:S(2)}) async-start(bf16[8,576,128]{2,1,0:T(8,128)(2,1)} %broadcast_in_dim.49), calls=%async_computation.4 | async-start | bytes 2359296 | tf_op jit(solution)/shard_map/all_to_all | solution.py:302
  221.5 16.3 %all-to-all-done.4 = bf16[8,576,128]{2,1,0:T(8,128)(2,1)S(1)} async-done(((bf16[8,576,128]{2,1,0:T(8,128)(2,1)}), bf16[8,576,128]{2,1,0:T(8,128)(2,1)S(1)}, u32[]{:S(2)}, u32[]{:S(2)}) %all-to-all-start.4) | async-done | bytes 1179680 | tf_op jit(solution)/shard_map/all_to_all | solution.py:302
  241.9 15.8 %all_to_all.36 = f32[8,64,128]{2,1,0:T(8,128)S(1)} all-to-all(f32[8,64,128]{2,1,0:T(8,128)S(1)} %bitcast.79), channel_id=1, replica_groups=mesh['z'=8,'xh'=2,'core'=2,'xl'=2,'y'=4] {'z'}, dimensions={0} | all-to-all | bytes 524288 | tf_op jit(solution)/shard_map/all_to_all | solution.py:309
  257.7 2.1 collective-permute-start.35
  259.8 2.3 collective-permute-done.35
  262.1 11.8 %all_to_all.37 = f32[8,64,128]{2,1,0:T(8,128)S(1)} all-to-all(f32[8,64,128]{2,1,0:T(8,128)S(1)} %broadcast_in_dim.50), channel_id=1, replica_groups=mesh['z'=8,'xh'=2,'core'=2,'xl'=2,'y'=4] {'z'}, dimensions={0} | all-to-all | bytes 524288 | tf_op jit(solution)/shard_map/all_to_all | solution.py:311
  273.9 4.0 %collective-permute-start.36 = (f32[512,128]{1,0:T(8,128)S(1)}, f32[512,128]{1,0:T(8,128)S(1)}, u32[]{:S(2)}, u32[]{:S(2)}) collective-permute-start(f32[512,128]{1,0:T(8,128)S(1)} %bitcast.77), channel_id=1, source_target_pairs={{0,8},{8,0},{1,9},{9,1},{2,10},{10,2},{3,11},{11,3},{4,12},{12,4},... | collective-permute-start | bytes 786440 | tf_op jit(solution)/shard_map/ppermute | solution.py:313
  (201 shorter events, 44.2 us)
Async XLA Ops:
  7.2 90.3 %all-gather.2.cloned.1.call-start = ((), (), s32[]{:S(2)}) async-start(), calls=%async_computation.7 | async-start | bytes 2654208 | tf_op jit(solution)/shard_map/all_gather | solution.py:254
  29.6 70.7 %all-to-all-start.1 = ((bf16[32,40,576]{2,1,0:T(8,128)(2,1)}), bf16[32,40,576]{2,1,0:T(8,128)(2,1)}, u32[]{:S(2)}, u32[]{:S(2)}) async-start(bf16[32,40,576]{2,1,0:T(8,128)(2,1)} %shard_map.104), calls=%async_computation.1 | async-start | bytes 3276800 | tf_op jit(solution)/shard_map/all_to_all | solution.py:255
  97.5 7.6 %collective-permute-start = (bf16[16,72,1024]{2,1,0:T(8,128)(2,1)}, bf16[16,72,1024]{2,1,0:T(8,128)(2,1)S(1)}, u32[]{:S(2)}, u32[]{:S(2)}) collective-permute-start(bf16[16,72,1024]{2,1,0:T(8,128)(2,1)} %all-gather.2.cloned.1.call-done.refs_0_.refs_2_.refs_4_.refs_6_.refs_8_.refs_10_.refs_12_.refs_14_.refs_16, ...), channel_id=1, source_target_pairs={{0,8},{8,0},{1,9},{9,1},{2,10},{10,2},{3,11},{11,3},{4,12},{12,4},... | collective-permute-start | bytes 7077896 | tf_op jit(solution)/shard_map/ppermute | solution.py:281
  116.4 20.4 %all-to-all-start.2 = ((bf16[8,72,1024]{2,1,0:T(8,128)(2,1)}), bf16[8,72,1024]{2,1,0:T(8,128)(2,1)S(1)}, u32[]{:S(2)}, u32[]{:S(2)}) async-start(bf16[8,72,1024]{2,1,0:T(8,128)(2,1)} %shard_map.106), calls=%async_computation.2 | async-start | bytes 2359296 | tf_op jit(solution)/shard_map/all_to_all | solution.py:291
  137.8 6.1 %collective-permute-start.2 = (bf16[72,1024]{1,0:T(8,128)(2,1)S(1)}, bf16[72,1024]{1,0:T(8,128)(2,1)S(1)}, u32[]{:S(2)}, u32[]{:S(2)}) collective-permute-start(bf16[72,1024]{1,0:T(8,128)(2,1)S(1)} %get-tuple-element.32.refs_0_.refs_32_), channel_id=1, source_target_pairs={{0,16},{16,0},{1,17},{17,1},{2,18},{18,2},{3,19},{19,3},{4,20},{20... | collective-permute-start | bytes 442376 | tf_op jit(solution)/shard_map/ppermute | solution.py:243
  139.8 6.7 %collective-permute-start.4 = (bf16[72,1024]{1,0:T(8,128)(2,1)S(1)}, bf16[72,1024]{1,0:T(8,128)(2,1)S(1)}, u32[]{:S(2)}, u32[]{:S(2)}) collective-permute-start(bf16[72,1024]{1,0:T(8,128)(2,1)S(1)} %get-tuple-element.32.refs_0_.refs_32_), channel_id=1, source_target_pairs={{0,32},{32,64},{64,96},{96,128},{128,160},{160,192},{192,224},{224... | collective-permute-start | bytes 442376 | tf_op jit(solution)/shard_map/ppermute | solution.py:24
  140.3 6.2 %collective-permute-start.17 = (bf16[72,1024]{1,0:T(8,128)(2,1)S(1)}, bf16[72,1024]{1,0:T(8,128)(2,1)S(1)}, u32[]{:S(2)}, u32[]{:S(2)}) collective-permute-start(bf16[72,1024]{1,0:T(8,128)(2,1)S(1)} %get-tuple-element.32.refs_0_.refs_32_), channel_id=1, source_target_pairs={{0,224},{32,0},{64,32},{96,64},{128,96},{160,128},{192,160},{224,1... | collective-permute-start | bytes 442376 | tf_op jit(solution)/shard_map/ppermute | solution.py:24
  143.9 5.4 %collective-permute-start.6 = (bf16[72,1024]{1,0:T(8,128)(2,1)S(1)}, bf16[72,1024]{1,0:T(8,128)(2,1)S(1)}, u32[]{:S(2)}, u32[]{:S(2)}) collective-permute-start(bf16[72,1024]{1,0:T(8,128)(2,1)S(1)} %collective-permute-done.2.refs_2_), channel_id=1, source_target_pairs={{0,32},{32,64},{64,96},{96,128},{128,160},{160,192},{192,224},{224... | collective-permute-start | bytes 442376 | tf_op jit(solution)/shard_map/ppermute | solution.py:24
  143.9 5.4 %collective-permute-start.23 = (bf16[72,1024]{1,0:T(8,128)(2,1)S(1)}, bf16[72,1024]{1,0:T(8,128)(2,1)S(1)}, u32[]{:S(2)}, u32[]{:S(2)}) collective-permute-start(bf16[72,1024]{1,0:T(8,128)(2,1)S(1)} %collective-permute-done.2.refs_2_), channel_id=1, source_target_pairs={{0,224},{32,0},{64,32},{96,64},{128,96},{160,128},{192,160},{224,1... | collective-permute-start | bytes 442376 | tf_op jit(solution)/shard_map/ppermute | solution.py:24
  146.6 6.2 %collective-permute-start.8 = (bf16[72,1024]{1,0:T(8,128)(2,1)S(1)}, bf16[72,1024]{1,0:T(8,128)(2,1)S(1)}, u32[]{:S(2)}, u32[]{:S(2)}) collective-permute-start(bf16[72,1024]{1,0:T(8,128)(2,1)S(1)} %collective-permute-done.4.refs_4_), channel_id=1, source_target_pairs={{0,32},{32,64},{64,96},{96,128},{128,160},{160,192},{192,224},{224... | collective-permute-start | bytes 442376 | tf_op jit(solution)/shard_map/ppermute | solution.py:24
  146.6 10.1 %collective-permute-start.18 = (bf16[72,1024]{1,0:T(8,128)(2,1)S(1)}, bf16[72,1024]{1,0:T(8,128)(2,1)S(1)}, u32[]{:S(2)}, u32[]{:S(2)}) collective-permute-start(bf16[72,1024]{1,0:T(8,128)(2,1)S(1)} %collective-permute-done.17.refs_28_), channel_id=1, source_target_pairs={{0,224},{32,0},{64,32},{96,64},{128,96},{160,128},{192,160},{224,1... | collective-permute-start | bytes 442376 | tf_op jit(solution)/shard_map/ppermute | solution.py:24
  149.3 10.4 %collective-permute-start.10 = (bf16[72,1024]{1,0:T(8,128)(2,1)S(1)}, bf16[72,1024]{1,0:T(8,128)(2,1)S(1)}, u32[]{:S(2)}, u32[]{:S(2)}) collective-permute-start(bf16[72,1024]{1,0:T(8,128)(2,1)S(1)} %collective-permute-done.6.refs_6_), channel_id=1, source_target_pairs={{0,32},{32,64},{64,96},{96,128},{128,160},{160,192},{192,224},{224... | collective-permute-start | bytes 442376 | tf_op jit(solution)/shard_map/ppermute | solution.py:24
  149.3 11.0 %collective-permute-start.24 = (bf16[72,1024]{1,0:T(8,128)(2,1)S(1)}, bf16[72,1024]{1,0:T(8,128)(2,1)S(1)}, u32[]{:S(2)}, u32[]{:S(2)}) collective-permute-start(bf16[72,1024]{1,0:T(8,128)(2,1)S(1)} %collective-permute-done.23.refs_30_), channel_id=1, source_target_pairs={{0,224},{32,0},{64,32},{96,64},{128,96},{160,128},{192,160},{224,1... | collective-permute-start | bytes 442376 | tf_op jit(solution)/shard_map/ppermute | solution.py:24
  152.8 7.5 %collective-permute-start.12 = (bf16[72,1024]{1,0:T(8,128)(2,1)S(1)}, bf16[72,1024]{1,0:T(8,128)(2,1)S(1)}, u32[]{:S(2)}, u32[]{:S(2)}) collective-permute-start(bf16[72,1024]{1,0:T(8,128)(2,1)S(1)} %collective-permute-done.8.refs_8_), channel_id=1, source_target_pairs={{0,32},{32,64},{64,96},{96,128},{128,160},{160,192},{192,224},{224... | collective-permute-start | bytes 442376 | tf_op jit(solution)/shard_map/ppermute | solution.py:24
  152.8 10.2 %collective-permute-start.1 = (bf16[72,1024]{1,0:T(8,128)(2,1)S(1)}, bf16[72,1024]{1,0:T(8,128)(2,1)S(1)}, u32[]{:S(2)}, u32[]{:S(2)}) collective-permute-start(bf16[72,1024]{1,0:T(8,128)(2,1)S(1)} %get-tuple-element.32.refs_0_.refs_32_), channel_id=1, source_target_pairs={{0,8},{8,0},{1,9},{9,1},{2,10},{10,2},{3,11},{11,3},{4,12},{12,4},... | collective-permute-start | bytes 442376 | tf_op jit(solution)/shard_map/ppermute | solution.py:248
  156.7 6.4 %collective-permute-start.19 = (bf16[72,1024]{1,0:T(8,128)(2,1)S(1)}, bf16[72,1024]{1,0:T(8,128)(2,1)S(1)}, u32[]{:S(2)}, u32[]{:S(2)}) collective-permute-start(bf16[72,1024]{1,0:T(8,128)(2,1)S(1)} %collective-permute-done.18.refs_24_), channel_id=1, source_target_pairs={{0,224},{32,0},{64,32},{96,64},{128,96},{160,128},{192,160},{224,1... | collective-permute-start | bytes 442376 | tf_op jit(solution)/shard_map/ppermute | solution.py:24
  159.6 5.5 %collective-permute-start.3 = (bf16[72,1024]{1,0:T(8,128)(2,1)S(1)}, bf16[72,1024]{1,0:T(8,128)(2,1)S(1)}, u32[]{:S(2)}, u32[]{:S(2)}) collective-permute-start(bf16[72,1024]{1,0:T(8,128)(2,1)S(1)} %collective-permute-done.2.refs_2_), channel_id=1, source_target_pairs={{0,8},{8,0},{1,9},{9,1},{2,10},{10,2},{3,11},{11,3},{4,12},{12,4},... | collective-permute-start | bytes 442376 | tf_op jit(solution)/shard_map/ppermute | solution.py:248
  160.2 9.2 %collective-permute-start.14 = (bf16[72,1024]{1,0:T(8,128)(2,1)S(1)}, bf16[72,1024]{1,0:T(8,128)(2,1)S(1)}, u32[]{:S(2)}, u32[]{:S(2)}) collective-permute-start(bf16[72,1024]{1,0:T(8,128)(2,1)S(1)} %collective-permute-done.10.refs_10_), channel_id=1, source_target_pairs={{0,32},{32,64},{64,96},{96,128},{128,160},{160,192},{192,224},{224... | collective-permute-start | bytes 442376 | tf_op jit(solution)/shard_map/ppermute | solution.py:24
  160.3 9.3 %collective-permute-start.25 = (bf16[72,1024]{1,0:T(8,128)(2,1)S(1)}, bf16[72,1024]{1,0:T(8,128)(2,1)S(1)}, u32[]{:S(2)}, u32[]{:S(2)}) collective-permute-start(bf16[72,1024]{1,0:T(8,128)(2,1)S(1)} %collective-permute-done.24.refs_26_), channel_id=1, source_target_pairs={{0,224},{32,0},{64,32},{96,64},{128,96},{160,128},{192,160},{224,1... | collective-permute-start | bytes 442376 | tf_op jit(solution)/shard_map/ppermute | solution.py:24
  163.0 5.4 %collective-permute-start.16 = (bf16[40,1024]{1,0:T(8,128)(2,1)S(1)}, bf16[40,1024]{1,0:T(8,128)(2,1)S(1)}, u32[]{:S(2)}, u32[]{:S(2)}) collective-permute-start(bf16[40,1024]{1,0:T(8,128)(2,1)S(1)} %slice.46), channel_id=1, source_target_pairs={{0,32},{32,64},{64,96},{96,128},{128,160},{160,192},{192,224},{224... | collective-permute-start | bytes 245768 | tf_op jit(solution)/shard_map/ppermute | solution.py:24
  163.1 6.6 %collective-permute-start.32 = (bf16[72,1024]{1,0:T(8,128)(2,1)S(1)}, bf16[72,1024]{1,0:T(8,128)(2,1)S(1)}, u32[]{:S(2)}, u32[]{:S(2)}) collective-permute-start(bf16[72,1024]{1,0:T(8,128)(2,1)S(1)} %collective-permute-done.17.refs_28_), channel_id=1, source_target_pairs={{0,8},{8,0},{1,9},{9,1},{2,10},{10,2},{3,11},{11,3},{4,12},{12,4},... | collective-permute-start | bytes 442376 | tf_op jit(solution)/shard_map/ppermute | solution.py:248
  165.2 8.8 %collective-permute-start.5 = (bf16[72,1024]{1,0:T(8,128)(2,1)S(1)}, bf16[72,1024]{1,0:T(8,128)(2,1)S(1)}, u32[]{:S(2)}, u32[]{:S(2)}) collective-permute-start(bf16[72,1024]{1,0:T(8,128)(2,1)S(1)} %collective-permute-done.4.refs_4_), channel_id=1, source_target_pairs={{0,8},{8,0},{1,9},{9,1},{2,10},{10,2},{3,11},{11,3},{4,12},{12,4},... | collective-permute-start | bytes 442376 | tf_op jit(solution)/shard_map/ppermute | solution.py:248
  168.4 7.9 %collective-permute-start.30 = (bf16[72,1024]{1,0:T(8,128)(2,1)S(1)}, bf16[72,1024]{1,0:T(8,128)(2,1)S(1)}, u32[]{:S(2)}, u32[]{:S(2)}) collective-permute-start(bf16[72,1024]{1,0:T(8,128)(2,1)S(1)} %collective-permute-done.18.refs_24_), channel_id=1, source_target_pairs={{0,8},{8,0},{1,9},{9,1},{2,10},{10,2},{3,11},{11,3},{4,12},{12,4},... | collective-permute-start | bytes 442376 | tf_op jit(solution)/shard_map/ppermute | solution.py:248
  169.5 6.9 %collective-permute-start.33 = (bf16[72,1024]{1,0:T(8,128)(2,1)S(1)}, bf16[72,1024]{1,0:T(8,128)(2,1)S(1)}, u32[]{:S(2)}, u32[]{:S(2)}) collective-permute-start(bf16[72,1024]{1,0:T(8,128)(2,1)S(1)} %collective-permute-done.23.refs_30_), channel_id=1, source_target_pairs={{0,8},{8,0},{1,9},{9,1},{2,10},{10,2},{3,11},{11,3},{4,12},{12,4},... | collective-permute-start | bytes 442376 | tf_op jit(solution)/shard_map/ppermute | solution.py:248
  169.6 3.1 %collective-permute-start.20 = (bf16[32,1024]{1,0:T(8,128)(2,1)S(1)}, bf16[32,1024]{1,0:T(8,128)(2,1)S(1)}, u32[]{:S(2)}, u32[]{:S(2)}) collective-permute-start(bf16[32,1024]{1,0:T(8,128)(2,1)S(1)} %slice.47), channel_id=1, source_target_pairs={{0,224},{32,0},{64,32},{96,64},{128,96},{160,128},{192,160},{224,1... | collective-permute-start | bytes 196616 | tf_op jit(solution)/shard_map/ppermute | solution.py:24
  169.7 8.9 %collective-permute-start.22 = (bf16[40,1024]{1,0:T(8,128)(2,1)S(1)}, bf16[40,1024]{1,0:T(8,128)(2,1)S(1)}, u32[]{:S(2)}, u32[]{:S(2)}) collective-permute-start(bf16[40,1024]{1,0:T(8,128)(2,1)S(1)} %slice.48), channel_id=1, source_target_pairs={{0,32},{32,64},{64,96},{96,128},{128,160},{160,192},{192,224},{224... | collective-permute-start | bytes 245768 | tf_op jit(solution)/shard_map/ppermute | solution.py:24
  172.7 4.1 %collective-permute-start.26 = (bf16[32,1024]{1,0:T(8,128)(2,1)S(1)}, bf16[32,1024]{1,0:T(8,128)(2,1)S(1)}, u32[]{:S(2)}, u32[]{:S(2)}) collective-permute-start(bf16[32,1024]{1,0:T(8,128)(2,1)S(1)} %slice.49), channel_id=1, source_target_pairs={{0,224},{32,0},{64,32},{96,64},{128,96},{160,128},{192,160},{224,1... | collective-permute-start | bytes 196616 | tf_op jit(solution)/shard_map/ppermute | solution.py:24
  174.0 4.6 %collective-permute-start.7 = (bf16[72,1024]{1,0:T(8,128)(2,1)S(1)}, bf16[72,1024]{1,0:T(8,128)(2,1)S(1)}, u32[]{:S(2)}, u32[]{:S(2)}) collective-permute-start(bf16[72,1024]{1,0:T(8,128)(2,1)S(1)} %collective-permute-done.6.refs_6_), channel_id=1, source_target_pairs={{0,8},{8,0},{1,9},{9,1},{2,10},{10,2},{3,11},{11,3},{4,12},{12,4},... | collective-permute-start | bytes 442376 | tf_op jit(solution)/shard_map/ppermute | solution.py:248
  191.1 23.2 %all-to-all-start.3 = ((bf16[8,720,128]{2,1,0:T(8,128)(2,1)}), bf16[8,720,128]{2,1,0:T(8,128)(2,1)S(1)}, u32[]{:S(2)}, u32[]{:S(2)}) async-start(bf16[8,720,128]{2,1,0:T(8,128)(2,1)} %shard_map.107), calls=%async_computation.3 | async-start | bytes 2949120 | tf_op jit(solution)/shard_map/all_to_all | solution.py:296
  217.8 20.0 %all-to-all-start.4 = ((bf16[8,576,128]{2,1,0:T(8,128)(2,1)}), bf16[8,576,128]{2,1,0:T(8,128)(2,1)S(1)}, u32[]{:S(2)}, u32[]{:S(2)}) async-start(bf16[8,576,128]{2,1,0:T(8,128)(2,1)} %broadcast_in_dim.49), calls=%async_computation.4 | async-start | bytes 2359296 | tf_op jit(solution)/shard_map/all_to_all | solution.py:302
  257.7 4.4 %collective-permute-start.35 = (f32[64,128]{1,0:T(8,128)S(1)}, f32[64,128]{1,0:T(8,128)S(1)}, u32[]{:S(2)}, u32[]{:S(2)}) collective-permute-start(f32[64,128]{1,0:T(8,128)S(1)} %reduce_sum.32), channel_id=1, source_target_pairs={{0,16},{16,0},{1,17},{17,1},{2,18},{18,2},{3,19},{19,3},{4,20},{20... | collective-permute-start | bytes 98312 | tf_op jit(solution)/shard_map/ppermute | solution.py:310
  273.9 5.2 %collective-permute-start.36 = (f32[512,128]{1,0:T(8,128)S(1)}, f32[512,128]{1,0:T(8,128)S(1)}, u32[]{:S(2)}, u32[]{:S(2)}) collective-permute-start(f32[512,128]{1,0:T(8,128)S(1)} %bitcast.77), channel_id=1, source_target_pairs={{0,8},{8,0},{1,9},{9,1},{2,10},{10,2},{3,11},{11,3},{4,12},{12,4},... | collective-permute-start | bytes 786440 | tf_op jit(solution)/shard_map/ppermute | solution.py:313
  (50 other events, 598.4 us)
Sparse Core Ops, SparseCore 0:
  24.6 72.8 all-gather.1

commit v2 on v1

--- a/solution.py
+++ b/solution.py
@@ -132,7 +132,7 @@
             out[c, 2 * PANEL :] = extra[:, columns]
 
 
-def product(weights, places, pieces, extra=(), width=256):
+def product(weights, places, pieces, extra=(), width=512):
     depth, rows = weights.shape
     by_rows = not extra
     if by_rows:

time: 288 us -> 286 us (level)
  no operation moved by 1% of the time
where the time goes in v2:
time: 286 us; the launch traced here: 284 us
  waiting for transfers between devices  83.6 us (29%)
  starting transfers between devices  66.8 us (23%)
  blocking collectives  42.5 us (15%)
  local copies, waits for them, and re-layouts  35.3 us (12%)
  Pallas kernels  29.4 us (10%)
  between operations  16.7 us (6%)
  other arithmetic  9.53 us (3%)
    optimization_barrier x1, local copies, waits for them, and re-layouts, local(): blocks, pair = lax.optimization_barrier((blocks, pair))  19.6 us
    all_to_all x1, waiting for transfers between devices, local(): lax.all_to_all(product(weights, places, pieces, (high, low)), COL, 0, 0,...  19.5 us
    ppermute x16, starting transfers between devices, hop(): return lax.ppermute(x, 'z', [(i, (i + k) % NZ) for i in range(NZ)])  19.1 us
    all_gather x1, waiting for transfers between devices, local(): gathered = lax.all_gather(pair, 'z', axis=0, tiled=True)  18.4 us
    all_to_all x1, waiting for transfers between devices, local(): lax.all_to_all(jnp.broadcast_to(x, (NZ,) + x.shape), COL, 0, 0, tiled=True)  16.3 us
    pallas_call x2, Pallas kernels, product(): pl.pallas_call(functools.partial(product_kernel, by_rows), grid_spec=pltp...  15.9 us
    all_to_all x1, blocking collectives, local(): lax.all_to_all(mine.reshape(NZ, 64, 128), 'z', 0, 0, tiled=True)  15.8 us
    all_to_all x1, waiting for transfers between devices, local(): lax.all_to_all(product(weights, places, pieces), COL, 0, 0, tiled=True)  15.6 us
  transfers between devices with their start and end apart: 42, of which 16 were waited for; matrix products, arithmetic and copies ran while one was open for 12% of the time, Pallas kernels for 5%

profile of v2, /device:TPU:1, one launch (start us, length us, event | category | flops | bytes accessed | tf_op | source)
XLA Modules:
  0.0 284.4 jit_solution(847957083335984518)
XLA Ops:
  8.8 14.9 %all_to_all.35 = bf16[16,72,128]{2,1,0:T(8,128)(2,1)S(1)} all-to-all(bf16[16,72,128]{2,1,0:T(8,128)(2,1)S(1)} %pad_maximum_fusion), channel_id=1, replica_groups=mesh['z'=8,'xh'=2,'core'=2,'xl'=2,'y'=4] {'xh','xl','y'}, dimensions={0} | all-to-all | bytes 589824 | tf_op jit(solution)/shard_map/all_to_all | solution.py:238
  25.2 4.4 %shard_map.104 = bf16[32,40,576]{2,1,0:T(8,128)(2,1)} custom-call(s32[32]{0:T(128)} %fold.1, s32[3]{0:T(128)} %pad_add_fusion.place, bf16[65,288,288]{2,1,0:T(8,128)(2,1)} %bitcast.68), custom_call_target="tpu_custom_call" | custom-call | bytes 6291456 | tf_op jit(solution)/shard_map/pallas_call | solution.py:99
  29.6 11.6 %all-to-all-start.1 = ((bf16[32,40,576]{2,1,0:T(8,128)(2,1)}), bf16[32,40,576]{2,1,0:T(8,128)(2,1)}, u32[]{:S(2)}, u32[]{:S(2)}) async-start(bf16[32,40,576]{2,1,0:T(8,128)(2,1)} %shard_map.104), calls=%async_computation.1 | async-start | bytes 3276800 | tf_op jit(solution)/shard_map/all_to_all | solution.py:255
  47.1 19.6 %copy.19 = bf16[65,288,288]{1,2,0:T(8,128)(2,1)} copy(bf16[65,288,288]{2,1,0:T(8,128)(2,1)} %bitcast.69) | data formatting | bytes 21565440 | tf_op jit(solution)/shard_map/optimization_barrier | solution.py:257
  66.7 1.8 dynamic-slice_bitcast_fusion
  74.8 4.2 %shard_map.103.own = bf16[32,72,576]{2,1,0:T(8,128)(2,1)} custom-call(s32[32]{0:T(128)} %get-tuple-element.36.below, s32[1]{0:T(128)} %bitcast.6.odd, bf16[32,40,288]{2,1,0:T(8,128)(2,1)} %broadcast_select_fusion.1.first, bf16[32,40,288]{2,1,0:T(8,128)(2,1)} %broadcast_select_fusion.second, f32[2,40,288]{2,1,0:T(8,128)} %maximum_convert_fusion.diagonal), custom_call_target="tpu_custom_call" | custom-call | bytes 6291456 | tf_op jit(solution)/shard_map/pallas_call | solution.py:214
  79.1 18.4 %all-gather.2.cloned.1.call-done.refs_0_.refs_2_.refs_4_.refs_6_.refs_8_.refs_10_.refs_12_.refs_14_.refs_16_.refs_18_.refs_20_.refs_22_.refs_24_.refs_26_.refs_28_.refs_30_ = bf16[16,72,1024]{2,1,0:T(8,128)(2,1)} async-done(((bf16[2,72,1024]{2,1,0:T(8,128)(2,1)}), bf16[16,72,1024]{2,1,0:T(8,128)(2,1)}) %all-gather.2.cloned.1.call-update) | async-done | bytes 2359312 | tf_op jit(solution)/shard_map/all_gather | solution.py:254
  100.3 4.9 %shard_map.105 = bf16[32,72,576]{2,1,0:T(8,128)(2,1)} custom-call(s32[32]{0:T(128)} %add.199.order, s32[32]{0:T(128)} %get-tuple-element.36.below, s32[1]{0:T(128)} %bitcast.6.odd, bf16[32,40,576]{2,1,0:T(8,128)(2,1)} %all-to-all-done.1.taken, bf16[32,72,576]{2,1,0:T(8,128)(2,1)} %shard_map.103.own), custom_call_target="tpu_custom_call" | custom-call | bytes 6291456 | tf_op jit(solution)/shard_map/pallas_call | solution.py:214
  106.6 8.3 %shard_map.106 = bf16[8,72,1024]{2,1,0:T(8,128)(2,1)} custom-call(s32[16]{0:T(128)} %add.203.places, bf16[2304,576]{1,0:T(8,128)(2,1)} %bitcast.71, bf16[16,72,1024]{2,1,0:T(8,128)(2,1)} %all-gather.2.cloned.1.call-done.refs_0_.refs_2_.refs_4_.refs_6_.refs_8_.refs_10_.refs_12_.refs_14_.refs_16_.refs_18_.refs_20_.refs_22_.refs_24_.refs_26_.refs_28_.refs_30_, ...), custom_call_target="tpu_custom_call" | custom-call | flops 2717908992 | bytes 9437184 | tf_op jit(solution)/shard_map/pallas_call | solution.py:151
  114.9 4.0 %all-to-all-start.2 = ((bf16[8,72,1024]{2,1,0:T(8,128)(2,1)}), bf16[8,72,1024]{2,1,0:T(8,128)(2,1)S(1)}, u32[]{:S(2)}, u32[]{:S(2)}) async-start(bf16[8,72,1024]{2,1,0:T(8,128)(2,1)} %shard_map.106), calls=%async_computation.2 | async-start | bytes 2359296 | tf_op jit(solution)/shard_map/all_to_all | solution.py:291
  119.7 15.6 %all-to-all-done.2 = bf16[8,72,1024]{2,1,0:T(8,128)(2,1)S(1)} async-done(((bf16[8,72,1024]{2,1,0:T(8,128)(2,1)}), bf16[8,72,1024]{2,1,0:T(8,128)(2,1)S(1)}, u32[]{:S(2)}, u32[]{:S(2)}) %all-to-all-start.2) | async-done | bytes 1179680 | tf_op jit(solution)/shard_map/all_to_all | solution.py:291
  136.3 2.1 collective-permute-start.2
  138.9 2.2 collective-permute-start.17
  142.4 2.7 collective-permute-start.23
  145.1 2.7 collective-permute-start.18
  147.8 2.7 collective-permute-start.24
  151.3 3.9 %collective-permute-start.1 = (bf16[72,1024]{1,0:T(8,128)(2,1)S(1)}, bf16[72,1024]{1,0:T(8,128)(2,1)S(1)}, u32[]{:S(2)}, u32[]{:S(2)}) collective-permute-start(bf16[72,1024]{1,0:T(8,128)(2,1)S(1)} %get-tuple-element.32.refs_0_.refs_32_), channel_id=1, source_target_pairs={{0,8},{8,0},{1,9},{9,1},{2,10},{10,2},{3,11},{11,3},{4,12},{12,4},... | collective-permute-start | bytes 442376 | tf_op jit(solution)/shard_map/ppermute | solution.py:248
  155.2 3.0 %collective-permute-start.19 = (bf16[72,1024]{1,0:T(8,128)(2,1)S(1)}, bf16[72,1024]{1,0:T(8,128)(2,1)S(1)}, u32[]{:S(2)}, u32[]{:S(2)}) collective-permute-start(bf16[72,1024]{1,0:T(8,128)(2,1)S(1)} %collective-permute-done.18.refs_24_), channel_id=1, source_target_pairs={{0,224},{32,0},{64,32},{96,64},{128,96},{160,128},{192,160},{224,1... | collective-permute-start | bytes 442376 | tf_op jit(solution)/shard_map/ppermute | solution.py:24
  158.8 2.7 collective-permute-start.25
  161.6 2.1 collective-permute-start.32
  163.8 3.1 %collective-permute-done.16 = bf16[40,1024]{1,0:T(8,128)(2,1)S(1)} collective-permute-done((bf16[40,1024]{1,0:T(8,128)(2,1)S(1)}, bf16[40,1024]{1,0:T(8,128)(2,1)S(1)}, u32[]{:S(2)}, u32[]{:S(2)}) %collective-permute-start.16) | collective-permute-done | bytes 81952 | tf_op jit(solution)/shard_map/ppermute | solution.py:24
  172.5 2.3 collective-permute-start.7
  181.2 7.6 %shard_map.107 = bf16[8,720,128]{2,1,0:T(8,128)(2,1)} custom-call(s32[16]{0:T(128)} %add.203.places, bf16[2304,576]{1,0:T(8,128)(2,1)} %bitcast.72, bf16[72,1024]{1,0:T(8,128)(2,1)} %copy-done.6, bf16[72,1024]{1,0:T(8,128)(2,1)} %copy-done.24, bf16[72,1024]{1,0:T(8,128)(2,1)} %copy-done.15, bf16[72,1024]{1,0:T(8,128)(2,1)} %copy-done.25, ...), custom_call_target="tpu_custom_call" | custom-call | flops 2717908992 | bytes 9437184 | tf_op jit(solution)/shard_map/pallas_call | solution.py:151
  188.8 3.7 %all-to-all-start.3 = ((bf16[8,720,128]{2,1,0:T(8,128)(2,1)}), bf16[8,720,128]{2,1,0:T(8,128)(2,1)S(1)}, u32[]{:S(2)}, u32[]{:S(2)}) async-start(bf16[8,720,128]{2,1,0:T(8,128)(2,1)} %shard_map.107), calls=%async_computation.3 | async-start | bytes 2949120 | tf_op jit(solution)/shard_map/all_to_all | solution.py:296
  192.6 19.5 %all-to-all-done.3 = bf16[8,720,128]{2,1,0:T(8,128)(2,1)S(1)} async-done(((bf16[8,720,128]{2,1,0:T(8,128)(2,1)}), bf16[8,720,128]{2,1,0:T(8,128)(2,1)S(1)}, u32[]{:S(2)}, u32[]{:S(2)}) %all-to-all-start.3) | async-done | bytes 1474592 | tf_op jit(solution)/shard_map/all_to_all | solution.py:296
  215.6 3.6 %all-to-all-start.4 = ((bf16[8,576,128]{2,1,0:T(8,128)(2,1)}), bf16[8,576,128]{2,1,0:T(8,128)(2,1)S(1)}, u32[]{:S(2)}, u32[]{:S(2)}) async-start(bf16[8,576,128]{2,1,0:T(8,128)(2,1)} %broadcast_in_dim.49), calls=%async_computation.4 | async-start | bytes 2359296 | tf_op jit(solution)/shard_map/all_to_all | solution.py:302
  219.2 16.3 %all-to-all-done.4 = bf16[8,576,128]{2,1,0:T(8,128)(2,1)S(1)} async-done(((bf16[8,576,128]{2,1,0:T(8,128)(2,1)}), bf16[8,576,128]{2,1,0:T(8,128)(2,1)S(1)}, u32[]{:S(2)}, u32[]{:S(2)}) %all-to-all-start.4) | async-done | bytes 1179680 | tf_op jit(solution)/shard_map/all_to_all | solution.py:302
  239.6 15.8 %all_to_all.36 = f32[8,64,128]{2,1,0:T(8,128)S(1)} all-to-all(f32[8,64,128]{2,1,0:T(8,128)S(1)} %bitcast.79), channel_id=1, replica_groups=mesh['z'=8,'xh'=2,'core'=2,'xl'=2,'y'=4] {'z'}, dimensions={0} | all-to-all | bytes 524288 | tf_op jit(solution)/shard_map/all_to_all | solution.py:309
  255.4 2.1 collective-permute-start.35
  257.5 2.3 collective-permute-done.35
  259.8 11.8 %all_to_all.37 = f32[8,64,128]{2,1,0:T(8,128)S(1)} all-to-all(f32[8,64,128]{2,1,0:T(8,128)S(1)} %broadcast_in_dim.50), channel_id=1, replica_groups=mesh['z'=8,'xh'=2,'core'=2,'xl'=2,'y'=4] {'z'}, dimensions={0} | all-to-all | bytes 524288 | tf_op jit(solution)/shard_map/all_to_all | solution.py:311
  271.6 4.0 %collective-permute-start.36 = (f32[512,128]{1,0:T(8,128)S(1)}, f32[512,128]{1,0:T(8,128)S(1)}, u32[]{:S(2)}, u32[]{:S(2)}) collective-permute-start(f32[512,128]{1,0:T(8,128)S(1)} %bitcast.77), channel_id=1, source_target_pairs={{0,8},{8,0},{1,9},{9,1},{2,10},{10,2},{3,11},{11,3},{4,12},{12,4},... | collective-permute-start | bytes 786440 | tf_op jit(solution)/shard_map/ppermute | solution.py:313
  (201 shorter events, 44.2 us)
Async XLA Ops:
  7.2 90.3 %all-gather.2.cloned.1.call-start = ((), (), s32[]{:S(2)}) async-start(), calls=%async_computation.7 | async-start | bytes 2654208 | tf_op jit(solution)/shard_map/all_gather | solution.py:254
  29.6 70.7 %all-to-all-start.1 = ((bf16[32,40,576]{2,1,0:T(8,128)(2,1)}), bf16[32,40,576]{2,1,0:T(8,128)(2,1)}, u32[]{:S(2)}, u32[]{:S(2)}) async-start(bf16[32,40,576]{2,1,0:T(8,128)(2,1)} %shard_map.104), calls=%async_computation.1 | async-start | bytes 3276800 | tf_op jit(solution)/shard_map/all_to_all | solution.py:255
  97.5 7.6 %collective-permute-start = (bf16[16,72,1024]{2,1,0:T(8,128)(2,1)}, bf16[16,72,1024]{2,1,0:T(8,128)(2,1)S(1)}, u32[]{:S(2)}, u32[]{:S(2)}) collective-permute-start(bf16[16,72,1024]{2,1,0:T(8,128)(2,1)} %all-gather.2.cloned.1.call-done.refs_0_.refs_2_.refs_4_.refs_6_.refs_8_.refs_10_.refs_12_.refs_14_.refs_16, ...), channel_id=1, source_target_pairs={{0,8},{8,0},{1,9},{9,1},{2,10},{10,2},{3,11},{11,3},{4,12},{12,4},... | collective-permute-start | bytes 7077896 | tf_op jit(solution)/shard_map/ppermute | solution.py:281
  114.9 20.4 %all-to-all-start.2 = ((bf16[8,72,1024]{2,1,0:T(8,128)(2,1)}), bf16[8,72,1024]{2,1,0:T(8,128)(2,1)S(1)}, u32[]{:S(2)}, u32[]{:S(2)}) async-start(bf16[8,72,1024]{2,1,0:T(8,128)(2,1)} %shard_map.106), calls=%async_computation.2 | async-start | bytes 2359296 | tf_op jit(solution)/shard_map/all_to_all | solution.py:291
  136.3 6.1 %collective-permute-start.2 = (bf16[72,1024]{1,0:T(8,128)(2,1)S(1)}, bf16[72,1024]{1,0:T(8,128)(2,1)S(1)}, u32[]{:S(2)}, u32[]{:S(2)}) collective-permute-start(bf16[72,1024]{1,0:T(8,128)(2,1)S(1)} %get-tuple-element.32.refs_0_.refs_32_), channel_id=1, source_target_pairs={{0,16},{16,0},{1,17},{17,1},{2,18},{18,2},{3,19},{19,3},{4,20},{20... | collective-permute-start | bytes 442376 | tf_op jit(solution)/shard_map/ppermute | solution.py:243
  138.3 6.7 %collective-permute-start.4 = (bf16[72,1024]{1,0:T(8,128)(2,1)S(1)}, bf16[72,1024]{1,0:T(8,128)(2,1)S(1)}, u32[]{:S(2)}, u32[]{:S(2)}) collective-permute-start(bf16[72,1024]{1,0:T(8,128)(2,1)S(1)} %get-tuple-element.32.refs_0_.refs_32_), channel_id=1, source_target_pairs={{0,32},{32,64},{64,96},{96,128},{128,160},{160,192},{192,224},{224... | collective-permute-start | bytes 442376 | tf_op jit(solution)/shard_map/ppermute | solution.py:24
  138.9 6.2 %collective-permute-start.17 = (bf16[72,1024]{1,0:T(8,128)(2,1)S(1)}, bf16[72,1024]{1,0:T(8,128)(2,1)S(1)}, u32[]{:S(2)}, u32[]{:S(2)}) collective-permute-start(bf16[72,1024]{1,0:T(8,128)(2,1)S(1)} %get-tuple-element.32.refs_0_.refs_32_), channel_id=1, source_target_pairs={{0,224},{32,0},{64,32},{96,64},{128,96},{160,128},{192,160},{224,1... | collective-permute-start | bytes 442376 | tf_op jit(solution)/shard_map/ppermute | solution.py:24
  142.4 5.4 %collective-permute-start.6 = (bf16[72,1024]{1,0:T(8,128)(2,1)S(1)}, bf16[72,1024]{1,0:T(8,128)(2,1)S(1)}, u32[]{:S(2)}, u32[]{:S(2)}) collective-permute-start(bf16[72,1024]{1,0:T(8,128)(2,1)S(1)} %collective-permute-done.2.refs_2_), channel_id=1, source_target_pairs={{0,32},{32,64},{64,96},{96,128},{128,160},{160,192},{192,224},{224... | collective-permute-start | bytes 442376 | tf_op jit(solution)/shard_map/ppermute | solution.py:24
  142.4 5.4 %collective-permute-start.23 = (bf16[72,1024]{1,0:T(8,128)(2,1)S(1)}, bf16[72,1024]{1,0:T(8,128)(2,1)S(1)}, u32[]{:S(2)}, u32[]{:S(2)}) collective-permute-start(bf16[72,1024]{1,0:T(8,128)(2,1)S(1)} %collective-permute-done.2.refs_2_), channel_id=1, source_target_pairs={{0,224},{32,0},{64,32},{96,64},{128,96},{160,128},{192,160},{224,1... | collective-permute-start | bytes 442376 | tf_op jit(solution)/shard_map/ppermute | solution.py:24
  145.1 6.2 %collective-permute-start.8 = (bf16[72,1024]{1,0:T(8,128)(2,1)S(1)}, bf16[72,1024]{1,0:T(8,128)(2,1)S(1)}, u32[]{:S(2)}, u32[]{:S(2)}) collective-permute-start(bf16[72,1024]{1,0:T(8,128)(2,1)S(1)} %collective-permute-done.4.refs_4_), channel_id=1, source_target_pairs={{0,32},{32,64},{64,96},{96,128},{128,160},{160,192},{192,224},{224... | collective-permute-start | bytes 442376 | tf_op jit(solution)/shard_map/ppermute | solution.py:24
  145.1 10.1 %collective-permute-start.18 = (bf16[72,1024]{1,0:T(8,128)(2,1)S(1)}, bf16[72,1024]{1,0:T(8,128)(2,1)S(1)}, u32[]{:S(2)}, u32[]{:S(2)}) collective-permute-start(bf16[72,1024]{1,0:T(8,128)(2,1)S(1)} %collective-permute-done.17.refs_28_), channel_id=1, source_target_pairs={{0,224},{32,0},{64,32},{96,64},{128,96},{160,128},{192,160},{224,1... | collective-permute-start | bytes 442376 | tf_op jit(solution)/shard_map/ppermute | solution.py:24
  147.8 10.4 %collective-permute-start.10 = (bf16[72,1024]{1,0:T(8,128)(2,1)S(1)}, bf16[72,1024]{1,0:T(8,128)(2,1)S(1)}, u32[]{:S(2)}, u32[]{:S(2)}) collective-permute-start(bf16[72,1024]{1,0:T(8,128)(2,1)S(1)} %collective-permute-done.6.refs_6_), channel_id=1, source_target_pairs={{0,32},{32,64},{64,96},{96,128},{128,160},{160,192},{192,224},{224... | collective-permute-start | bytes 442376 | tf_op jit(solution)/shard_map/ppermute | solution.py:24
  147.8 11.0 %collective-permute-start.24 = (bf16[72,1024]{1,0:T(8,128)(2,1)S(1)}, bf16[72,1024]{1,0:T(8,128)(2,1)S(1)}, u32[]{:S(2)}, u32[]{:S(2)}) collective-permute-start(bf16[72,1024]{1,0:T(8,128)(2,1)S(1)} %collective-permute-done.23.refs_30_), channel_id=1, source_target_pairs={{0,224},{32,0},{64,32},{96,64},{128,96},{160,128},{192,160},{224,1... | collective-permute-start | bytes 442376 | tf_op jit(solution)/shard_map/ppermute | solution.py:24
  151.3 7.5 %collective-permute-start.12 = (bf16[72,1024]{1,0:T(8,128)(2,1)S(1)}, bf16[72,1024]{1,0:T(8,128)(2,1)S(1)}, u32[]{:S(2)}, u32[]{:S(2)}) collective-permute-start(bf16[72,1024]{1,0:T(8,128)(2,1)S(1)} %collective-permute-done.8.refs_8_), channel_id=1, source_target_pairs={{0,32},{32,64},{64,96},{96,128},{128,160},{160,192},{192,224},{224... | collective-permute-start | bytes 442376 | tf_op jit(solution)/shard_map/ppermute | solution.py:24
  151.3 10.2 %collective-permute-start.1 = (bf16[72,1024]{1,0:T(8,128)(2,1)S(1)}, bf16[72,1024]{1,0:T(8,128)(2,1)S(1)}, u32[]{:S(2)}, u32[]{:S(2)}) collective-permute-start(bf16[72,1024]{1,0:T(8,128)(2,1)S(1)} %get-tuple-element.32.refs_0_.refs_32_), channel_id=1, source_target_pairs={{0,8},{8,0},{1,9},{9,1},{2,10},{10,2},{3,11},{11,3},{4,12},{12,4},... | collective-permute-start | bytes 442376 | tf_op jit(solution)/shard_map/ppermute | solution.py:248
  155.2 6.4 %collective-permute-start.19 = (bf16[72,1024]{1,0:T(8,128)(2,1)S(1)}, bf16[72,1024]{1,0:T(8,128)(2,1)S(1)}, u32[]{:S(2)}, u32[]{:S(2)}) collective-permute-start(bf16[72,1024]{1,0:T(8,128)(2,1)S(1)} %collective-permute-done.18.refs_24_), channel_id=1, source_target_pairs={{0,224},{32,0},{64,32},{96,64},{128,96},{160,128},{192,160},{224,1... | collective-permute-start | bytes 442376 | tf_op jit(solution)/shard_map/ppermute | solution.py:24
  158.2 5.5 %collective-permute-start.3 = (bf16[72,1024]{1,0:T(8,128)(2,1)S(1)}, bf16[72,1024]{1,0:T(8,128)(2,1)S(1)}, u32[]{:S(2)}, u32[]{:S(2)}) collective-permute-start(bf16[72,1024]{1,0:T(8,128)(2,1)S(1)} %collective-permute-done.2.refs_2_), channel_id=1, source_target_pairs={{0,8},{8,0},{1,9},{9,1},{2,10},{10,2},{3,11},{11,3},{4,12},{12,4},... | collective-permute-start | bytes 442376 | tf_op jit(solution)/shard_map/ppermute | solution.py:248
  158.8 9.2 %collective-permute-start.14 = (bf16[72,1024]{1,0:T(8,128)(2,1)S(1)}, bf16[72,1024]{1,0:T(8,128)(2,1)S(1)}, u32[]{:S(2)}, u32[]{:S(2)}) collective-permute-start(bf16[72,1024]{1,0:T(8,128)(2,1)S(1)} %collective-permute-done.10.refs_10_), channel_id=1, source_target_pairs={{0,32},{32,64},{64,96},{96,128},{128,160},{160,192},{192,224},{224... | collective-permute-start | bytes 442376 | tf_op jit(solution)/shard_map/ppermute | solution.py:24
  158.8 9.3 %collective-permute-start.25 = (bf16[72,1024]{1,0:T(8,128)(2,1)S(1)}, bf16[72,1024]{1,0:T(8,128)(2,1)S(1)}, u32[]{:S(2)}, u32[]{:S(2)}) collective-permute-start(bf16[72,1024]{1,0:T(8,128)(2,1)S(1)} %collective-permute-done.24.refs_26_), channel_id=1, source_target_pairs={{0,224},{32,0},{64,32},{96,64},{128,96},{160,128},{192,160},{224,1... | collective-permute-start | bytes 442376 | tf_op jit(solution)/shard_map/ppermute | solution.py:24
  161.5 5.4 %collective-permute-start.16 = (bf16[40,1024]{1,0:T(8,128)(2,1)S(1)}, bf16[40,1024]{1,0:T(8,128)(2,1)S(1)}, u32[]{:S(2)}, u32[]{:S(2)}) collective-permute-start(bf16[40,1024]{1,0:T(8,128)(2,1)S(1)} %slice.46), channel_id=1, source_target_pairs={{0,32},{32,64},{64,96},{96,128},{128,160},{160,192},{192,224},{224... | collective-permute-start | bytes 245768 | tf_op jit(solution)/shard_map/ppermute | solution.py:24
  161.6 6.6 %collective-permute-start.32 = (bf16[72,1024]{1,0:T(8,128)(2,1)S(1)}, bf16[72,1024]{1,0:T(8,128)(2,1)S(1)}, u32[]{:S(2)}, u32[]{:S(2)}) collective-permute-start(bf16[72,1024]{1,0:T(8,128)(2,1)S(1)} %collective-permute-done.17.refs_28_), channel_id=1, source_target_pairs={{0,8},{8,0},{1,9},{9,1},{2,10},{10,2},{3,11},{11,3},{4,12},{12,4},... | collective-permute-start | bytes 442376 | tf_op jit(solution)/shard_map/ppermute | solution.py:248
  163.7 8.8 %collective-permute-start.5 = (bf16[72,1024]{1,0:T(8,128)(2,1)S(1)}, bf16[72,1024]{1,0:T(8,128)(2,1)S(1)}, u32[]{:S(2)}, u32[]{:S(2)}) collective-permute-start(bf16[72,1024]{1,0:T(8,128)(2,1)S(1)} %collective-permute-done.4.refs_4_), channel_id=1, source_target_pairs={{0,8},{8,0},{1,9},{9,1},{2,10},{10,2},{3,11},{11,3},{4,12},{12,4},... | collective-permute-start | bytes 442376 | tf_op jit(solution)/shard_map/ppermute | solution.py:248
  166.9 7.9 %collective-permute-start.30 = (bf16[72,1024]{1,0:T(8,128)(2,1)S(1)}, bf16[72,1024]{1,0:T(8,128)(2,1)S(1)}, u32[]{:S(2)}, u32[]{:S(2)}) collective-permute-start(bf16[72,1024]{1,0:T(8,128)(2,1)S(1)} %collective-permute-done.18.refs_24_), channel_id=1, source_target_pairs={{0,8},{8,0},{1,9},{9,1},{2,10},{10,2},{3,11},{11,3},{4,12},{12,4},... | collective-permute-start | bytes 442376 | tf_op jit(solution)/shard_map/ppermute | solution.py:248
  168.0 6.9 %collective-permute-start.33 = (bf16[72,1024]{1,0:T(8,128)(2,1)S(1)}, bf16[72,1024]{1,0:T(8,128)(2,1)S(1)}, u32[]{:S(2)}, u32[]{:S(2)}) collective-permute-start(bf16[72,1024]{1,0:T(8,128)(2,1)S(1)} %collective-permute-done.23.refs_30_), channel_id=1, source_target_pairs={{0,8},{8,0},{1,9},{9,1},{2,10},{10,2},{3,11},{11,3},{4,12},{12,4},... | collective-permute-start | bytes 442376 | tf_op jit(solution)/shard_map/ppermute | solution.py:248
  168.1 3.1 %collective-permute-start.20 = (bf16[32,1024]{1,0:T(8,128)(2,1)S(1)}, bf16[32,1024]{1,0:T(8,128)(2,1)S(1)}, u32[]{:S(2)}, u32[]{:S(2)}) collective-permute-start(bf16[32,1024]{1,0:T(8,128)(2,1)S(1)} %slice.47), channel_id=1, source_target_pairs={{0,224},{32,0},{64,32},{96,64},{128,96},{160,128},{192,160},{224,1... | collective-permute-start | bytes 196616 | tf_op jit(solution)/shard_map/ppermute | solution.py:24
  168.2 8.9 %collective-permute-start.22 = (bf16[40,1024]{1,0:T(8,128)(2,1)S(1)}, bf16[40,1024]{1,0:T(8,128)(2,1)S(1)}, u32[]{:S(2)}, u32[]{:S(2)}) collective-permute-start(bf16[40,1024]{1,0:T(8,128)(2,1)S(1)} %slice.48), channel_id=1, source_target_pairs={{0,32},{32,64},{64,96},{96,128},{128,160},{160,192},{192,224},{224... | collective-permute-start | bytes 245768 | tf_op jit(solution)/shard_map/ppermute | solution.py:24
  171.2 4.1 %collective-permute-start.26 = (bf16[32,1024]{1,0:T(8,128)(2,1)S(1)}, bf16[32,1024]{1,0:T(8,128)(2,1)S(1)}, u32[]{:S(2)}, u32[]{:S(2)}) collective-permute-start(bf16[32,1024]{1,0:T(8,128)(2,1)S(1)} %slice.49), channel_id=1, source_target_pairs={{0,224},{32,0},{64,32},{96,64},{128,96},{160,128},{192,160},{224,1... | collective-permute-start | bytes 196616 | tf_op jit(solution)/shard_map/ppermute | solution.py:24
  172.5 4.6 %collective-permute-start.7 = (bf16[72,1024]{1,0:T(8,128)(2,1)S(1)}, bf16[72,1024]{1,0:T(8,128)(2,1)S(1)}, u32[]{:S(2)}, u32[]{:S(2)}) collective-permute-start(bf16[72,1024]{1,0:T(8,128)(2,1)S(1)} %collective-permute-done.6.refs_6_), channel_id=1, source_target_pairs={{0,8},{8,0},{1,9},{9,1},{2,10},{10,2},{3,11},{11,3},{4,12},{12,4},... | collective-permute-start | bytes 442376 | tf_op jit(solution)/shard_map/ppermute | solution.py:248
  188.8 23.2 %all-to-all-start.3 = ((bf16[8,720,128]{2,1,0:T(8,128)(2,1)}), bf16[8,720,128]{2,1,0:T(8,128)(2,1)S(1)}, u32[]{:S(2)}, u32[]{:S(2)}) async-start(bf16[8,720,128]{2,1,0:T(8,128)(2,1)} %shard_map.107), calls=%async_computation.3 | async-start | bytes 2949120 | tf_op jit(solution)/shard_map/all_to_all | solution.py:296
  215.6 20.0 %all-to-all-start.4 = ((bf16[8,576,128]{2,1,0:T(8,128)(2,1)}), bf16[8,576,128]{2,1,0:T(8,128)(2,1)S(1)}, u32[]{:S(2)}, u32[]{:S(2)}) async-start(bf16[8,576,128]{2,1,0:T(8,128)(2,1)} %broadcast_in_dim.49), calls=%async_computation.4 | async-start | bytes 2359296 | tf_op jit(solution)/shard_map/all_to_all | solution.py:302
  255.4 4.4 %collective-permute-start.35 = (f32[64,128]{1,0:T(8,128)S(1)}, f32[64,128]{1,0:T(8,128)S(1)}, u32[]{:S(2)}, u32[]{:S(2)}) collective-permute-start(f32[64,128]{1,0:T(8,128)S(1)} %reduce_sum.32), channel_id=1, source_target_pairs={{0,16},{16,0},{1,17},{17,1},{2,18},{18,2},{3,19},{19,3},{4,20},{20... | collective-permute-start | bytes 98312 | tf_op jit(solution)/shard_map/ppermute | solution.py:310
  271.6 5.2 %collective-permute-start.36 = (f32[512,128]{1,0:T(8,128)S(1)}, f32[512,128]{1,0:T(8,128)S(1)}, u32[]{:S(2)}, u32[]{:S(2)}) collective-permute-start(f32[512,128]{1,0:T(8,128)S(1)} %bitcast.77), channel_id=1, source_target_pairs={{0,8},{8,0},{1,9},{9,1},{2,10},{10,2},{3,11},{11,3},{4,12},{12,4},... | collective-permute-start | bytes 786440 | tf_op jit(solution)/shard_map/ppermute | solution.py:313
  (50 other events, 598.4 us)
Sparse Core Ops, SparseCore 0:
  24.6 72.8 all-gather.1

commit v3 on v2

--- a/solution.py
+++ b/solution.py
@@ -54,12 +54,6 @@
     x = x.reshape((SHARE, 8) + x.shape[1:])
     x = jnp.take(x, row_order(), axis=0)
     return x.reshape((NZ, SHARE) + x.shape[2:])
-
-
-def merge_rows(x):
-    x = x.reshape((SHARE, 8) + x.shape[2:])
-    x = jnp.take(x, np.argsort(row_order()), axis=0)
-    return x.reshape((2 * PANEL,) + x.shape[2:])
 
 
 def window_kernel(fold, place, blocks, out, held, sems):
@@ -222,6 +216,55 @@
     )(*scalars, *arrays)
 
 
+def finish_kernel(parts, shift_rows, first, second, wide):
+    total = parts[0, : 2 * PANEL].astype(jnp.float32)
+    for c in range(1, NZ):
+        total += parts[c, : 2 * PANEL].astype(jnp.float32)
+    tails = [parts[c, 2 * PANEL :].astype(jnp.float32) for c in range(NZ)]
+
+    def natural(offset):
+        upper, lower = [], []
+        for tail, (_, n0, _, _) in zip(tails, shares()):
+            upper.append(tail[offset : offset + n0])
+            lower.append(tail[offset + n0 : offset + SHARE])
+        return jnp.concatenate(upper + lower)
+
+    high = natural(0)
+    first[...] = high + natural(SHARE)
+    result = total + shift_rows[...] * high
+    second[...] = result
+    for c in range(NZ):
+        wide[c] = result.astype(wide.dtype)
+
+
+def finish(parts, shift_rows):
+    image = jax.ShapeDtypeStruct((2 * PANEL, 128), jnp.float32)
+    return pl.pallas_call(
+        finish_kernel,
+        in_specs=[pl.BlockSpec(memory_space=pltpu.VMEM)] * 2,
+        out_specs=[pl.BlockSpec(memory_space=pltpu.VMEM)] * 3,
+        out_shape=[image, image, jax.ShapeDtypeStruct((NZ, 2 * PANEL, 128), jnp.bfloat16)],
+        compiler_params=pltpu.CompilerParams(vmem_limit_bytes=48 * 2**20),
+    )(parts, shift_rows)
+
+
+def gram_kernel(rows, x, out):
+    for c in range(NZ):
+        out[c] = lax.dot_general(
+            rows[c], x[...], (((0,), (0,)), ((), ())), preferred_element_type=jnp.float32
+        )
+
+
+def gram_part(rows, x):
+    return pl.pallas_call(
+        gram_kernel,
+        in_specs=[pl.BlockSpec(memory_space=pltpu.VMEM)] * 2,
+        out_specs=pl.BlockSpec(memory_space=pltpu.VMEM),
+        out_shape=jax.ShapeDtypeStruct((NZ, 128, 128), jnp.float32),
+        compiler_params=pltpu.CompilerParams(vmem_limit_bytes=48 * 2**20),
+    )(rows, x)
+
+
 def local(corner_blocks, diag_shift, sketch, panel_fold):
     z = lax.axis_index("z")
     core = lax.axis_index("core")
@@ -294,14 +337,9 @@
     high, low = rounded.astype(jnp.bfloat16), (share - rounded).astype(jnp.bfloat16)
     pieces = gather_operand(high)
     parts = lax.all_to_all(product(weights, places, pieces, (high, low)), COL, 0, 0, tiled=True)
-    x = merge_rows(parts[:, 2 * PANEL : 2 * PANEL + SHARE]).astype(jnp.float32)
-    first = x + merge_rows(parts[:, 2 * PANEL + SHARE :]).astype(jnp.float32)
-    second = jnp.sum(parts[:, : 2 * PANEL].astype(jnp.float32), axis=0) + shift_rows * x
-    x = second.astype(jnp.bfloat16)
-
-    rows = lax.all_to_all(jnp.broadcast_to(x, (NZ,) + x.shape), COL, 0, 0, tiled=True)
-    rows, first, second = lax.optimization_barrier((rows, first, second))
-    part = lax.dot_general(rows, x, (((1,), (0,)), ((), ())), preferred_element_type=jnp.float32)
+    first, second, wide = finish(parts, shift_rows)
+    rows = lax.all_to_all(wide, COL, 0, 0, tiled=True)
+    part = gram_part(rows, wide[0])
     part = part.reshape(2, 512, 128)
     mine = lax.dynamic_index_in_dim(part, core, 0, keepdims=False)
     theirs = lax.dynamic_index_in_dim(part, 1 - core, 0, keepdims=False)

time: 286 us -> 282 us (0.986)
  no operation moved by 1% of the time
where the time goes in v3:
time: 282 us; the launch traced here: 281 us
  waiting for transfers between devices  82.2 us (29%)
  starting transfers between devices  66.9 us (24%)
  blocking collectives  42.4 us (15%)
  local copies, waits for them, and re-layouts  32.8 us (12%)
  Pallas kernels  31.4 us (11%)
  between operations  16.7 us (6%)
  other arithmetic  8.57 us (3%)
    optimization_barrier x1, local copies, waits for them, and re-layouts, local(): blocks, pair = lax.optimization_barrier((blocks, pair))  19.6 us
    all_to_all x1, waiting for transfers between devices, local(): lax.all_to_all(product(weights, places, pieces, (high, low)), COL, 0, 0,...  19.3 us
    ppermute x16, starting transfers between devices, hop(): return lax.ppermute(x, 'z', [(i, (i + k) % NZ) for i in range(NZ)])  19.1 us
    all_gather x1, waiting for transfers between devices, local(): gathered = lax.all_gather(pair, 'z', axis=0, tiled=True)  18.2 us
    pallas_call x2, Pallas kernels, product(): pl.pallas_call(functools.partial(product_kernel, by_rows), grid_spec=pltp...  15.9 us
    all_to_all x1, blocking collectives, local(): lax.all_to_all(mine.reshape(NZ, 64, 128), 'z', 0, 0, tiled=True)  15.7 us
    all_to_all x1, waiting for transfers between devices, local(): lax.all_to_all(product(weights, places, pieces), COL, 0, 0, tiled=True)  15.6 us
    all_to_all x1, waiting for transfers between devices, local(): rows = lax.all_to_all(wide, COL, 0, 0, tiled=True)  15.4 us
  transfers between devices with their start and end apart: 42, of which 16 were waited for; matrix products, arithmetic and copies ran while one was open for 12% of the time, Pallas kernels for 5%

profile of v3, /device:TPU:1, one launch (start us, length us, event | category | flops | bytes accessed | tf_op | source)
XLA Modules:
  0.0 280.8 jit_solution(2992423112146221071)
XLA Ops:
  8.8 14.9 %all_to_all.35 = bf16[16,72,128]{2,1,0:T(8,128)(2,1)S(1)} all-to-all(bf16[16,72,128]{2,1,0:T(8,128)(2,1)S(1)} %pad_maximum_fusion), channel_id=1, replica_groups=mesh['z'=8,'xh'=2,'core'=2,'xl'=2,'y'=4] {'xh','xl','y'}, dimensions={0} | all-to-all | bytes 589824 | tf_op jit(solution)/shard_map/all_to_all | solution.py:281
  25.2 4.4 %shard_map.86 = bf16[32,40,576]{2,1,0:T(8,128)(2,1)} custom-call(s32[32]{0:T(128)} %fold.1, s32[3]{0:T(128)} %pad_add_fusion.place, bf16[65,288,288]{2,1,0:T(8,128)(2,1)} %bitcast.46), custom_call_target="tpu_custom_call" | custom-call | bytes 6291456 | tf_op jit(solution)/shard_map/pallas_call | solution.py:93
  29.6 11.6 %all-to-all-start.1 = ((bf16[32,40,576]{2,1,0:T(8,128)(2,1)}), bf16[32,40,576]{2,1,0:T(8,128)(2,1)}, u32[]{:S(2)}, u32[]{:S(2)}) async-start(bf16[32,40,576]{2,1,0:T(8,128)(2,1)} %shard_map.86), calls=%async_computation.1 | async-start | bytes 3276800 | tf_op jit(solution)/shard_map/all_to_all | solution.py:298
  47.3 19.6 %copy.17 = bf16[65,288,288]{1,2,0:T(8,128)(2,1)} copy(bf16[65,288,288]{2,1,0:T(8,128)(2,1)} %bitcast.47) | data formatting | bytes 21565440 | tf_op jit(solution)/shard_map/optimization_barrier | solution.py:300
  66.9 1.8 dynamic-slice_bitcast_fusion
  75.0 4.2 %shard_map.85.own = bf16[32,72,576]{2,1,0:T(8,128)(2,1)} custom-call(s32[32]{0:T(128)} %get-tuple-element.30.below, s32[1]{0:T(128)} %bitcast.6.odd, bf16[32,40,288]{2,1,0:T(8,128)(2,1)} %broadcast_select_fusion.1.first, bf16[32,40,288]{2,1,0:T(8,128)(2,1)} %broadcast_select_fusion.second, f32[2,40,288]{2,1,0:T(8,128)} %maximum_convert_fusion.diagonal), custom_call_target="tpu_custom_call" | custom-call | bytes 6291456 | tf_op jit(solution)/shard_map/pallas_call | solution.py:208
  79.3 18.2 %all-gather.2.cloned.1.call-done.refs_0_.refs_2_.refs_4_.refs_6_.refs_8_.refs_10_.refs_12_.refs_14_.refs_16_.refs_18_.refs_20_.refs_22_.refs_24_.refs_26_.refs_28_.refs_30_ = bf16[16,72,1024]{2,1,0:T(8,128)(2,1)} async-done(((bf16[2,72,1024]{2,1,0:T(8,128)(2,1)}), bf16[16,72,1024]{2,1,0:T(8,128)(2,1)}) %all-gather.2.cloned.1.call-update) | async-done | bytes 2359312 | tf_op jit(solution)/shard_map/all_gather | solution.py:297
  100.3 4.9 %shard_map.87 = bf16[32,72,576]{2,1,0:T(8,128)(2,1)} custom-call(s32[32]{0:T(128)} %add.192.order, s32[32]{0:T(128)} %get-tuple-element.30.below, s32[1]{0:T(128)} %bitcast.6.odd, bf16[32,40,576]{2,1,0:T(8,128)(2,1)} %all-to-all-done.1.taken, bf16[32,72,576]{2,1,0:T(8,128)(2,1)} %shard_map.85.own), custom_call_target="tpu_custom_call" | custom-call | bytes 6291456 | tf_op jit(solution)/shard_map/pallas_call | solution.py:208
  106.6 8.3 %shard_map.88 = bf16[8,72,1024]{2,1,0:T(8,128)(2,1)} custom-call(s32[16]{0:T(128)} %add.196.places, bf16[2304,576]{1,0:T(8,128)(2,1)} %bitcast.49, bf16[16,72,1024]{2,1,0:T(8,128)(2,1)} %all-gather.2.cloned.1.call-done.refs_0_.refs_2_.refs_4_.refs_6_.refs_8_.refs_10_.refs_12_.refs_14_.refs_16_.refs_18_.refs_20_.refs_22_.refs_24_.refs_26_.refs_28_.refs_30_, ...), custom_call_target="tpu_custom_call" | custom-call | flops 2717908992 | bytes 9437184 | tf_op jit(solution)/shard_map/pallas_call | solution.py:145
  114.9 3.9 %all-to-all-start.2 = ((bf16[8,72,1024]{2,1,0:T(8,128)(2,1)}), bf16[8,72,1024]{2,1,0:T(8,128)(2,1)S(1)}, u32[]{:S(2)}, u32[]{:S(2)}) async-start(bf16[8,72,1024]{2,1,0:T(8,128)(2,1)} %shard_map.88), calls=%async_computation.2 | async-start | bytes 2359296 | tf_op jit(solution)/shard_map/all_to_all | solution.py:334
  119.6 15.6 %all-to-all-done.2 = bf16[8,72,1024]{2,1,0:T(8,128)(2,1)S(1)} async-done(((bf16[8,72,1024]{2,1,0:T(8,128)(2,1)}), bf16[8,72,1024]{2,1,0:T(8,128)(2,1)S(1)}, u32[]{:S(2)}, u32[]{:S(2)}) %all-to-all-start.2) | async-done | bytes 1179680 | tf_op jit(solution)/shard_map/all_to_all | solution.py:334
  136.3 2.1 collective-permute-start.2
  138.9 2.2 collective-permute-start.17
  142.4 2.7 collective-permute-start.23
  145.1 2.7 collective-permute-start.18
  147.8 2.7 collective-permute-start.24
  151.3 3.9 %collective-permute-start.1 = (bf16[72,1024]{1,0:T(8,128)(2,1)S(1)}, bf16[72,1024]{1,0:T(8,128)(2,1)S(1)}, u32[]{:S(2)}, u32[]{:S(2)}) collective-permute-start(bf16[72,1024]{1,0:T(8,128)(2,1)S(1)} %get-tuple-element.27.refs_0_.refs_32_), channel_id=1, source_target_pairs={{0,8},{8,0},{1,9},{9,1},{2,10},{10,2},{3,11},{11,3},{4,12},{12,4},... | collective-permute-start | bytes 442376 | tf_op jit(solution)/shard_map/ppermute | solution.py:291
  155.2 3.0 %collective-permute-start.19 = (bf16[72,1024]{1,0:T(8,128)(2,1)S(1)}, bf16[72,1024]{1,0:T(8,128)(2,1)S(1)}, u32[]{:S(2)}, u32[]{:S(2)}) collective-permute-start(bf16[72,1024]{1,0:T(8,128)(2,1)S(1)} %collective-permute-done.18.refs_24_), channel_id=1, source_target_pairs={{0,224},{32,0},{64,32},{96,64},{128,96},{160,128},{192,160},{224,1... | collective-permute-start | bytes 442376 | tf_op jit(solution)/shard_map/ppermute | solution.py:24
  158.8 2.7 collective-permute-start.25
  161.6 2.1 collective-permute-start.32
  163.8 3.1 %collective-permute-done.16 = bf16[40,1024]{1,0:T(8,128)(2,1)S(1)} collective-permute-done((bf16[40,1024]{1,0:T(8,128)(2,1)S(1)}, bf16[40,1024]{1,0:T(8,128)(2,1)S(1)}, u32[]{:S(2)}, u32[]{:S(2)}) %collective-permute-start.16) | collective-permute-done | bytes 81952 | tf_op jit(solution)/shard_map/ppermute | solution.py:24
  172.5 2.3 collective-permute-start.7
  181.2 7.6 %shard_map.89 = bf16[8,720,128]{2,1,0:T(8,128)(2,1)} custom-call(s32[16]{0:T(128)} %add.196.places, bf16[2304,576]{1,0:T(8,128)(2,1)} %bitcast.50, bf16[72,1024]{1,0:T(8,128)(2,1)} %copy-done.6, bf16[72,1024]{1,0:T(8,128)(2,1)} %copy-done.23, bf16[72,1024]{1,0:T(8,128)(2,1)} %copy-done.14, bf16[72,1024]{1,0:T(8,128)(2,1)} %copy-done.24, ...), custom_call_target="tpu_custom_call" | custom-call | flops 2717908992 | bytes 9437184 | tf_op jit(solution)/shard_map/pallas_call | solution.py:145
  188.8 3.7 %all-to-all-start.3 = ((bf16[8,720,128]{2,1,0:T(8,128)(2,1)}), bf16[8,720,128]{2,1,0:T(8,128)(2,1)S(1)}, u32[]{:S(2)}, u32[]{:S(2)}) async-start(bf16[8,720,128]{2,1,0:T(8,128)(2,1)} %shard_map.89), calls=%async_computation.3 | async-start | bytes 2949120 | tf_op jit(solution)/shard_map/all_to_all | solution.py:339
  192.7 19.3 %all-to-all-done.3.parts = bf16[8,720,128]{2,1,0:T(8,128)(2,1)S(1)} async-done(((bf16[8,720,128]{2,1,0:T(8,128)(2,1)}), bf16[8,720,128]{2,1,0:T(8,128)(2,1)S(1)}, u32[]{:S(2)}, u32[]{:S(2)}) %all-to-all-start.3) | async-done | bytes 1474592 | tf_op jit(solution)/shard_map/all_to_all | solution.py:339
  213.4 3.6 %all-to-all-start.4 = ((bf16[8,576,128]{2,1,0:T(8,128)(2,1)}), bf16[8,576,128]{2,1,0:T(8,128)(2,1)S(1)}, u32[]{:S(2)}, u32[]{:S(2)}) async-start(bf16[8,576,128]{2,1,0:T(8,128)(2,1)} %get-tuple-element.19), calls=%async_computation.4 | async-start | bytes 2359296 | tf_op jit(solution)/shard_map/all_to_all | solution.py:341
  218.0 15.4 %all-to-all-done.4.rows = bf16[8,576,128]{2,1,0:T(8,128)(2,1)S(1)} async-done(((bf16[8,576,128]{2,1,0:T(8,128)(2,1)}), bf16[8,576,128]{2,1,0:T(8,128)(2,1)S(1)}, u32[]{:S(2)}, u32[]{:S(2)}) %all-to-all-start.4) | async-done | bytes 1179680 | tf_op jit(solution)/shard_map/all_to_all | solution.py:341
  236.1 15.7 %all_to_all.36 = f32[8,64,128]{2,1,0:T(8,128)S(1)} all-to-all(f32[8,64,128]{2,1,0:T(8,128)S(1)} %bitcast.56), channel_id=1, replica_groups=mesh['z'=8,'xh'=2,'core'=2,'xl'=2,'y'=4] {'z'}, dimensions={0} | all-to-all | bytes 524288 | tf_op jit(solution)/shard_map/all_to_all | solution.py:347
  251.8 2.2 collective-permute-start.35
  254.0 2.2 collective-permute-done.35
  256.2 11.8 %all_to_all.37 = f32[8,64,128]{2,1,0:T(8,128)S(1)} all-to-all(f32[8,64,128]{2,1,0:T(8,128)S(1)} %broadcast_in_dim.61), channel_id=1, replica_groups=mesh['z'=8,'xh'=2,'core'=2,'xl'=2,'y'=4] {'z'}, dimensions={0} | all-to-all | bytes 524288 | tf_op jit(solution)/shard_map/all_to_all | solution.py:349
  268.0 4.0 %collective-permute-start.36 = (f32[512,128]{1,0:T(8,128)S(1)}, f32[512,128]{1,0:T(8,128)S(1)}, u32[]{:S(2)}, u32[]{:S(2)}) collective-permute-start(f32[512,128]{1,0:T(8,128)S(1)} %bitcast.54), channel_id=1, source_target_pairs={{0,8},{8,0},{1,9},{9,1},{2,10},{10,2},{3,11},{11,3},{4,12},{12,4},... | collective-permute-start | bytes 786440 | tf_op jit(solution)/shard_map/ppermute | solution.py:351
  (192 shorter events, 41.9 us)
Async XLA Ops:
  7.2 90.3 %all-gather.2.cloned.1.call-start = ((), (), s32[]{:S(2)}) async-start(), calls=%async_computation.7 | async-start | bytes 2654208 | tf_op jit(solution)/shard_map/all_gather | solution.py:297
  29.6 70.7 %all-to-all-start.1 = ((bf16[32,40,576]{2,1,0:T(8,128)(2,1)}), bf16[32,40,576]{2,1,0:T(8,128)(2,1)}, u32[]{:S(2)}, u32[]{:S(2)}) async-start(bf16[32,40,576]{2,1,0:T(8,128)(2,1)} %shard_map.86), calls=%async_computation.1 | async-start | bytes 3276800 | tf_op jit(solution)/shard_map/all_to_all | solution.py:298
  97.5 7.7 %collective-permute-start = (bf16[16,72,1024]{2,1,0:T(8,128)(2,1)}, bf16[16,72,1024]{2,1,0:T(8,128)(2,1)S(1)}, u32[]{:S(2)}, u32[]{:S(2)}) collective-permute-start(bf16[16,72,1024]{2,1,0:T(8,128)(2,1)} %all-gather.2.cloned.1.call-done.refs_0_.refs_2_.refs_4_.refs_6_.refs_8_.refs_10_.refs_12_.refs_14_.refs_16, ...), channel_id=1, source_target_pairs={{0,8},{8,0},{1,9},{9,1},{2,10},{10,2},{3,11},{11,3},{4,12},{12,4},... | collective-permute-start | bytes 7077896 | tf_op jit(solution)/shard_map/ppermute | solution.py:324
  114.9 20.4 %all-to-all-start.2 = ((bf16[8,72,1024]{2,1,0:T(8,128)(2,1)}), bf16[8,72,1024]{2,1,0:T(8,128)(2,1)S(1)}, u32[]{:S(2)}, u32[]{:S(2)}) async-start(bf16[8,72,1024]{2,1,0:T(8,128)(2,1)} %shard_map.88), calls=%async_computation.2 | async-start | bytes 2359296 | tf_op jit(solution)/shard_map/all_to_all | solution.py:334
  136.3 6.1 %collective-permute-start.2 = (bf16[72,1024]{1,0:T(8,128)(2,1)S(1)}, bf16[72,1024]{1,0:T(8,128)(2,1)S(1)}, u32[]{:S(2)}, u32[]{:S(2)}) collective-permute-start(bf16[72,1024]{1,0:T(8,128)(2,1)S(1)} %get-tuple-element.27.refs_0_.refs_32_), channel_id=1, source_target_pairs={{0,16},{16,0},{1,17},{17,1},{2,18},{18,2},{3,19},{19,3},{4,20},{20... | collective-permute-start | bytes 442376 | tf_op jit(solution)/shard_map/ppermute | solution.py:286
  138.4 6.7 %collective-permute-start.4 = (bf16[72,1024]{1,0:T(8,128)(2,1)S(1)}, bf16[72,1024]{1,0:T(8,128)(2,1)S(1)}, u32[]{:S(2)}, u32[]{:S(2)}) collective-permute-start(bf16[72,1024]{1,0:T(8,128)(2,1)S(1)} %get-tuple-element.27.refs_0_.refs_32_), channel_id=1, source_target_pairs={{0,32},{32,64},{64,96},{96,128},{128,160},{160,192},{192,224},{224... | collective-permute-start | bytes 442376 | tf_op jit(solution)/shard_map/ppermute | solution.py:24
  138.9 6.2 %collective-permute-start.17 = (bf16[72,1024]{1,0:T(8,128)(2,1)S(1)}, bf16[72,1024]{1,0:T(8,128)(2,1)S(1)}, u32[]{:S(2)}, u32[]{:S(2)}) collective-permute-start(bf16[72,1024]{1,0:T(8,128)(2,1)S(1)} %get-tuple-element.27.refs_0_.refs_32_), channel_id=1, source_target_pairs={{0,224},{32,0},{64,32},{96,64},{128,96},{160,128},{192,160},{224,1... | collective-permute-start | bytes 442376 | tf_op jit(solution)/shard_map/ppermute | solution.py:24
  142.4 5.4 %collective-permute-start.6 = (bf16[72,1024]{1,0:T(8,128)(2,1)S(1)}, bf16[72,1024]{1,0:T(8,128)(2,1)S(1)}, u32[]{:S(2)}, u32[]{:S(2)}) collective-permute-start(bf16[72,1024]{1,0:T(8,128)(2,1)S(1)} %collective-permute-done.2.refs_2_), channel_id=1, source_target_pairs={{0,32},{32,64},{64,96},{96,128},{128,160},{160,192},{192,224},{224... | collective-permute-start | bytes 442376 | tf_op jit(solution)/shard_map/ppermute | solution.py:24
  142.4 5.4 %collective-permute-start.23 = (bf16[72,1024]{1,0:T(8,128)(2,1)S(1)}, bf16[72,1024]{1,0:T(8,128)(2,1)S(1)}, u32[]{:S(2)}, u32[]{:S(2)}) collective-permute-start(bf16[72,1024]{1,0:T(8,128)(2,1)S(1)} %collective-permute-done.2.refs_2_), channel_id=1, source_target_pairs={{0,224},{32,0},{64,32},{96,64},{128,96},{160,128},{192,160},{224,1... | collective-permute-start | bytes 442376 | tf_op jit(solution)/shard_map/ppermute | solution.py:24
  145.1 6.2 %collective-permute-start.8 = (bf16[72,1024]{1,0:T(8,128)(2,1)S(1)}, bf16[72,1024]{1,0:T(8,128)(2,1)S(1)}, u32[]{:S(2)}, u32[]{:S(2)}) collective-permute-start(bf16[72,1024]{1,0:T(8,128)(2,1)S(1)} %collective-permute-done.4.refs_4_), channel_id=1, source_target_pairs={{0,32},{32,64},{64,96},{96,128},{128,160},{160,192},{192,224},{224... | collective-permute-start | bytes 442376 | tf_op jit(solution)/shard_map/ppermute | solution.py:24
  145.1 10.1 %collective-permute-start.18 = (bf16[72,1024]{1,0:T(8,128)(2,1)S(1)}, bf16[72,1024]{1,0:T(8,128)(2,1)S(1)}, u32[]{:S(2)}, u32[]{:S(2)}) collective-permute-start(bf16[72,1024]{1,0:T(8,128)(2,1)S(1)} %collective-permute-done.17.refs_28_), channel_id=1, source_target_pairs={{0,224},{32,0},{64,32},{96,64},{128,96},{160,128},{192,160},{224,1... | collective-permute-start | bytes 442376 | tf_op jit(solution)/shard_map/ppermute | solution.py:24
  147.8 10.4 %collective-permute-start.10 = (bf16[72,1024]{1,0:T(8,128)(2,1)S(1)}, bf16[72,1024]{1,0:T(8,128)(2,1)S(1)}, u32[]{:S(2)}, u32[]{:S(2)}) collective-permute-start(bf16[72,1024]{1,0:T(8,128)(2,1)S(1)} %collective-permute-done.6.refs_6_), channel_id=1, source_target_pairs={{0,32},{32,64},{64,96},{96,128},{128,160},{160,192},{192,224},{224... | collective-permute-start | bytes 442376 | tf_op jit(solution)/shard_map/ppermute | solution.py:24
  147.8 11.0 %collective-permute-start.24 = (bf16[72,1024]{1,0:T(8,128)(2,1)S(1)}, bf16[72,1024]{1,0:T(8,128)(2,1)S(1)}, u32[]{:S(2)}, u32[]{:S(2)}) collective-permute-start(bf16[72,1024]{1,0:T(8,128)(2,1)S(1)} %collective-permute-done.23.refs_30_), channel_id=1, source_target_pairs={{0,224},{32,0},{64,32},{96,64},{128,96},{160,128},{192,160},{224,1... | collective-permute-start | bytes 442376 | tf_op jit(solution)/shard_map/ppermute | solution.py:24
  151.3 7.5 %collective-permute-start.12 = (bf16[72,1024]{1,0:T(8,128)(2,1)S(1)}, bf16[72,1024]{1,0:T(8,128)(2,1)S(1)}, u32[]{:S(2)}, u32[]{:S(2)}) collective-permute-start(bf16[72,1024]{1,0:T(8,128)(2,1)S(1)} %collective-permute-done.8.refs_8_), channel_id=1, source_target_pairs={{0,32},{32,64},{64,96},{96,128},{128,160},{160,192},{192,224},{224... | collective-permute-start | bytes 442376 | tf_op jit(solution)/shard_map/ppermute | solution.py:24
  151.3 10.2 %collective-permute-start.1 = (bf16[72,1024]{1,0:T(8,128)(2,1)S(1)}, bf16[72,1024]{1,0:T(8,128)(2,1)S(1)}, u32[]{:S(2)}, u32[]{:S(2)}) collective-permute-start(bf16[72,1024]{1,0:T(8,128)(2,1)S(1)} %get-tuple-element.27.refs_0_.refs_32_), channel_id=1, source_target_pairs={{0,8},{8,0},{1,9},{9,1},{2,10},{10,2},{3,11},{11,3},{4,12},{12,4},... | collective-permute-start | bytes 442376 | tf_op jit(solution)/shard_map/ppermute | solution.py:291
  155.2 6.4 %collective-permute-start.19 = (bf16[72,1024]{1,0:T(8,128)(2,1)S(1)}, bf16[72,1024]{1,0:T(8,128)(2,1)S(1)}, u32[]{:S(2)}, u32[]{:S(2)}) collective-permute-start(bf16[72,1024]{1,0:T(8,128)(2,1)S(1)} %collective-permute-done.18.refs_24_), channel_id=1, source_target_pairs={{0,224},{32,0},{64,32},{96,64},{128,96},{160,128},{192,160},{224,1... | collective-permute-start | bytes 442376 | tf_op jit(solution)/shard_map/ppermute | solution.py:24
  158.1 5.5 %collective-permute-start.3 = (bf16[72,1024]{1,0:T(8,128)(2,1)S(1)}, bf16[72,1024]{1,0:T(8,128)(2,1)S(1)}, u32[]{:S(2)}, u32[]{:S(2)}) collective-permute-start(bf16[72,1024]{1,0:T(8,128)(2,1)S(1)} %collective-permute-done.2.refs_2_), channel_id=1, source_target_pairs={{0,8},{8,0},{1,9},{9,1},{2,10},{10,2},{3,11},{11,3},{4,12},{12,4},... | collective-permute-start | bytes 442376 | tf_op jit(solution)/shard_map/ppermute | solution.py:291
  158.8 9.2 %collective-permute-start.14 = (bf16[72,1024]{1,0:T(8,128)(2,1)S(1)}, bf16[72,1024]{1,0:T(8,128)(2,1)S(1)}, u32[]{:S(2)}, u32[]{:S(2)}) collective-permute-start(bf16[72,1024]{1,0:T(8,128)(2,1)S(1)} %collective-permute-done.10.refs_10_), channel_id=1, source_target_pairs={{0,32},{32,64},{64,96},{96,128},{128,160},{160,192},{192,224},{224... | collective-permute-start | bytes 442376 | tf_op jit(solution)/shard_map/ppermute | solution.py:24
  158.8 9.3 %collective-permute-start.25 = (bf16[72,1024]{1,0:T(8,128)(2,1)S(1)}, bf16[72,1024]{1,0:T(8,128)(2,1)S(1)}, u32[]{:S(2)}, u32[]{:S(2)}) collective-permute-start(bf16[72,1024]{1,0:T(8,128)(2,1)S(1)} %collective-permute-done.24.refs_26_), channel_id=1, source_target_pairs={{0,224},{32,0},{64,32},{96,64},{128,96},{160,128},{192,160},{224,1... | collective-permute-start | bytes 442376 | tf_op jit(solution)/shard_map/ppermute | solution.py:24
  161.5 5.4 %collective-permute-start.16 = (bf16[40,1024]{1,0:T(8,128)(2,1)S(1)}, bf16[40,1024]{1,0:T(8,128)(2,1)S(1)}, u32[]{:S(2)}, u32[]{:S(2)}) collective-permute-start(bf16[40,1024]{1,0:T(8,128)(2,1)S(1)} %slice.34), channel_id=1, source_target_pairs={{0,32},{32,64},{64,96},{96,128},{128,160},{160,192},{192,224},{224... | collective-permute-start | bytes 245768 | tf_op jit(solution)/shard_map/ppermute | solution.py:24
  161.6 6.6 %collective-permute-start.32 = (bf16[72,1024]{1,0:T(8,128)(2,1)S(1)}, bf16[72,1024]{1,0:T(8,128)(2,1)S(1)}, u32[]{:S(2)}, u32[]{:S(2)}) collective-permute-start(bf16[72,1024]{1,0:T(8,128)(2,1)S(1)} %collective-permute-done.17.refs_28_), channel_id=1, source_target_pairs={{0,8},{8,0},{1,9},{9,1},{2,10},{10,2},{3,11},{11,3},{4,12},{12,4},... | collective-permute-start | bytes 442376 | tf_op jit(solution)/shard_map/ppermute | solution.py:291
  163.7 8.8 %collective-permute-start.5 = (bf16[72,1024]{1,0:T(8,128)(2,1)S(1)}, bf16[72,1024]{1,0:T(8,128)(2,1)S(1)}, u32[]{:S(2)}, u32[]{:S(2)}) collective-permute-start(bf16[72,1024]{1,0:T(8,128)(2,1)S(1)} %collective-permute-done.4.refs_4_), channel_id=1, source_target_pairs={{0,8},{8,0},{1,9},{9,1},{2,10},{10,2},{3,11},{11,3},{4,12},{12,4},... | collective-permute-start | bytes 442376 | tf_op jit(solution)/shard_map/ppermute | solution.py:291
  166.9 7.9 %collective-permute-start.30 = (bf16[72,1024]{1,0:T(8,128)(2,1)S(1)}, bf16[72,1024]{1,0:T(8,128)(2,1)S(1)}, u32[]{:S(2)}, u32[]{:S(2)}) collective-permute-start(bf16[72,1024]{1,0:T(8,128)(2,1)S(1)} %collective-permute-done.18.refs_24_), channel_id=1, source_target_pairs={{0,8},{8,0},{1,9},{9,1},{2,10},{10,2},{3,11},{11,3},{4,12},{12,4},... | collective-permute-start | bytes 442376 | tf_op jit(solution)/shard_map/ppermute | solution.py:291
  168.0 6.9 %collective-permute-start.33 = (bf16[72,1024]{1,0:T(8,128)(2,1)S(1)}, bf16[72,1024]{1,0:T(8,128)(2,1)S(1)}, u32[]{:S(2)}, u32[]{:S(2)}) collective-permute-start(bf16[72,1024]{1,0:T(8,128)(2,1)S(1)} %collective-permute-done.23.refs_30_), channel_id=1, source_target_pairs={{0,8},{8,0},{1,9},{9,1},{2,10},{10,2},{3,11},{11,3},{4,12},{12,4},... | collective-permute-start | bytes 442376 | tf_op jit(solution)/shard_map/ppermute | solution.py:291
  168.1 3.1 %collective-permute-start.20 = (bf16[32,1024]{1,0:T(8,128)(2,1)S(1)}, bf16[32,1024]{1,0:T(8,128)(2,1)S(1)}, u32[]{:S(2)}, u32[]{:S(2)}) collective-permute-start(bf16[32,1024]{1,0:T(8,128)(2,1)S(1)} %slice.35), channel_id=1, source_target_pairs={{0,224},{32,0},{64,32},{96,64},{128,96},{160,128},{192,160},{224,1... | collective-permute-start | bytes 196616 | tf_op jit(solution)/shard_map/ppermute | solution.py:24
  168.2 8.9 %collective-permute-start.22 = (bf16[40,1024]{1,0:T(8,128)(2,1)S(1)}, bf16[40,1024]{1,0:T(8,128)(2,1)S(1)}, u32[]{:S(2)}, u32[]{:S(2)}) collective-permute-start(bf16[40,1024]{1,0:T(8,128)(2,1)S(1)} %slice.36), channel_id=1, source_target_pairs={{0,32},{32,64},{64,96},{96,128},{128,160},{160,192},{192,224},{224... | collective-permute-start | bytes 245768 | tf_op jit(solution)/shard_map/ppermute | solution.py:24
  171.2 4.1 %collective-permute-start.26 = (bf16[32,1024]{1,0:T(8,128)(2,1)S(1)}, bf16[32,1024]{1,0:T(8,128)(2,1)S(1)}, u32[]{:S(2)}, u32[]{:S(2)}) collective-permute-start(bf16[32,1024]{1,0:T(8,128)(2,1)S(1)} %slice.37), channel_id=1, source_target_pairs={{0,224},{32,0},{64,32},{96,64},{128,96},{160,128},{192,160},{224,1... | collective-permute-start | bytes 196616 | tf_op jit(solution)/shard_map/ppermute | solution.py:24
  172.5 4.6 %collective-permute-start.7 = (bf16[72,1024]{1,0:T(8,128)(2,1)S(1)}, bf16[72,1024]{1,0:T(8,128)(2,1)S(1)}, u32[]{:S(2)}, u32[]{:S(2)}) collective-permute-start(bf16[72,1024]{1,0:T(8,128)(2,1)S(1)} %collective-permute-done.6.refs_6_), channel_id=1, source_target_pairs={{0,8},{8,0},{1,9},{9,1},{2,10},{10,2},{3,11},{11,3},{4,12},{12,4},... | collective-permute-start | bytes 442376 | tf_op jit(solution)/shard_map/ppermute | solution.py:291
  188.8 23.2 %all-to-all-start.3 = ((bf16[8,720,128]{2,1,0:T(8,128)(2,1)}), bf16[8,720,128]{2,1,0:T(8,128)(2,1)S(1)}, u32[]{:S(2)}, u32[]{:S(2)}) async-start(bf16[8,720,128]{2,1,0:T(8,128)(2,1)} %shard_map.89), calls=%async_computation.3 | async-start | bytes 2949120 | tf_op jit(solution)/shard_map/all_to_all | solution.py:339
  213.4 20.0 %all-to-all-start.4 = ((bf16[8,576,128]{2,1,0:T(8,128)(2,1)}), bf16[8,576,128]{2,1,0:T(8,128)(2,1)S(1)}, u32[]{:S(2)}, u32[]{:S(2)}) async-start(bf16[8,576,128]{2,1,0:T(8,128)(2,1)} %get-tuple-element.19), calls=%async_computation.4 | async-start | bytes 2359296 | tf_op jit(solution)/shard_map/all_to_all | solution.py:341
  251.8 4.4 %collective-permute-start.35 = (f32[64,128]{1,0:T(8,128)S(1)}, f32[64,128]{1,0:T(8,128)S(1)}, u32[]{:S(2)}, u32[]{:S(2)}) collective-permute-start(f32[64,128]{1,0:T(8,128)S(1)} %reduce_sum.19), channel_id=1, source_target_pairs={{0,16},{16,0},{1,17},{17,1},{2,18},{18,2},{3,19},{19,3},{4,20},{20... | collective-permute-start | bytes 98312 | tf_op jit(solution)/shard_map/ppermute | solution.py:348
  268.0 5.2 %collective-permute-start.36 = (f32[512,128]{1,0:T(8,128)S(1)}, f32[512,128]{1,0:T(8,128)S(1)}, u32[]{:S(2)}, u32[]{:S(2)}) collective-permute-start(f32[512,128]{1,0:T(8,128)S(1)} %bitcast.54), channel_id=1, source_target_pairs={{0,8},{8,0},{1,9},{9,1},{2,10},{10,2},{3,11},{11,3},{4,12},{12,4},... | collective-permute-start | bytes 786440 | tf_op jit(solution)/shard_map/ppermute | solution.py:351
  (49 other events, 594.8 us)
Sparse Core Ops, SparseCore 0:
  24.6 72.7 all-gather.1
